TPU v7x, 512 devices: a whole 4x4x16 slice. The times are simulated.
512 devices in a mesh: bl: 128 (over y, z, core), ch: 4 (over x).
Axes of the slice: x: 4, y: 4, z: 16, core: 2. Of those that a mesh axis runs over, the one named last changes fastest.
Arguments:
- sky_model_visibility: bfloat16 [2, 16384, 2048], P(None, 'bl', 'ch'), may hold values from -1 to 1
- measured_visibility: float32 [2, 16384, 64], P(None, 'bl', 'ch'), may hold values from -6 to 6
- rejected_cell_tally: int32 [16384, 64], P('bl', 'ch'), may hold values from 0 to 16
- station_pair_index: int32 [16384, 2], P('bl'), may hold values from 0 to 63, as said below
- fetch_lists: int32 [128, 64], replicated, may hold values from 0 to 511, as said below
- gain_values: float32 [2, 512, 2048], P(None, 'bl', 'ch'), may hold values from -5 to 5
- first_moment: float32 [2, 512, 2048], P(None, 'bl', 'ch'), may hold values from -0.3 to 0.3
- second_moment: float32 [2, 512, 2048], P(None, 'bl', 'ch'), may hold values from 0.004 to 0.02
Outputs:
- new_gains: float32 [2, 512, 2048], P(None, 'bl', 'ch')
- new_first: float32 [2, 512, 2048], P(None, 'bl', 'ch')
- new_second: float32 [2, 512, 2048], P(None, 'bl', 'ch')
- residual: float32 [2, 16384, 64], P(None, 'bl', 'ch')
Inputs may be any that keep to these rules, and one draw needn't show every extreme that they name: `fetch_lists`: entries of one row are distinct stations; a row takes exactly 1 stations from each block of 4 consecutive stations that it touches. `station_pair_index`: in each block of 128 rows, every row holds two positions i < j, and no pair repeats within the block.
All inputs are finite; a program needn't handle non-finite values.
Results may differ from a plain program's by a relative error of at most 0.00035.
Values sent between devices are 32-bit elements; how exact they have to be, the bound alone decides.
A program may use at most 64 MiB of HBM per device.

v0:
```python
import math

import jax
import jax.numpy as jnp
from jax import lax
from jax.sharding import PartitionSpec as P

SKY_SOURCES = 32
CELL_READINGS = 16
ITERS = 2
STEP = 3


BETA_ONE = 0.9
BETA_TWO = 0.99
ADAM_EPSILON = 1e-08
LEARN_RATE = 0.3
BLEND = 0.5
HIGHEST = lax.Precision.HIGHEST


def channel_kernel(nchan):
    chans = jnp.arange(nchan, dtype=jnp.float32)
    dist = jnp.abs(chans[:, None] - chans[None, :])
    raw = jnp.exp(-dist / (0.5 * nchan))
    return raw / jnp.sum(raw, axis=1, keepdims=True)


def residual_terms(
    gain_first,
    gain_second,
    sky_model_visibility,
    measured_visibility,
    reliability_scale,
    spectral_blend_weight,
):
    a = gain_first[0]
    b = gain_first[1]
    c = gain_second[0]
    d = gain_second[1]
    coh_real = sky_model_visibility[0].astype(jnp.float32)
    coh_imag = sky_model_visibility[1].astype(jnp.float32)
    u = a * c + b * d
    v = b * c - a * d
    rows_here = a.shape[0]
    model_real = jnp.sum((u * coh_real - v * coh_imag).reshape(rows_here, -1, SKY_SOURCES), axis=2)
    model_imag = jnp.sum((u * coh_imag + v * coh_real).reshape(rows_here, -1, SKY_SOURCES), axis=2)
    err_real = reliability_scale * (measured_visibility[0] - model_real)
    err_imag = reliability_scale * (measured_visibility[1] - model_imag)
    wide = (rows_here, err_real.shape[1], SKY_SOURCES)
    spread_real = jnp.broadcast_to(err_real[:, :, None], wide).reshape(rows_here, -1)
    spread_imag = jnp.broadcast_to(err_imag[:, :, None], wide).reshape(rows_here, -1)
    x = c * coh_real + d * coh_imag
    y = d * coh_real - c * coh_imag
    grad_first = spectral_blend_weight * jnp.stack(
        [spread_real * x - spread_imag * y, spread_real * y + spread_imag * x]
    )
    x = a * coh_real - b * coh_imag
    y = a * coh_imag + b * coh_real
    grad_second = spectral_blend_weight * jnp.stack(
        [spread_real * x + spread_imag * y, spread_real * y - spread_imag * x]
    )
    return (jnp.stack([err_real, err_imag]), grad_first, grad_second)


def adam_update(current, moment_one, moment_two, smoothed, tally_number):
    moment_one = BETA_ONE * moment_one + (1.0 - BETA_ONE) * smoothed
    moment_two = BETA_TWO * moment_two + (1.0 - BETA_TWO) * smoothed * smoothed
    first_hat = moment_one / (1.0 - BETA_ONE**tally_number)
    second_hat = moment_two / (1.0 - BETA_TWO**tally_number)
    current = current - LEARN_RATE * first_hat / (jnp.sqrt(second_hat) + ADAM_EPSILON)
    return (current, moment_one, moment_two)


def on_device(
    sky_model_visibility,
    measured_visibility,
    rejected_cell_tally,
    station_pair_index,
    fetch_lists,
    gain_values,
    first_moment,
    second_moment,
):
    baseline_count = lax.axis_size("bl")
    own_index = lax.axis_index("bl")
    ch_index = lax.axis_index("ch")
    own_count = gain_values.shape[1]
    width_dev = gain_values.shape[2]
    chan_dev = width_dev // SKY_SOURCES
    station_list = own_count * baseline_count
    baseline_list = station_pair_index.shape[0] * baseline_count
    spectral_blend_weight = -2.0 / math.sqrt(2.0 * baseline_list / station_list)
    fetched_count = fetch_lists.shape[1]
    kernel = channel_kernel(chan_dev * lax.axis_size("ch"))
    slot_ids = jnp.arange(fetched_count, dtype=jnp.int32)
    my_fetch = lax.dynamic_index_in_dim(fetch_lists, own_index, 0, keepdims=False)
    pick_first = (station_pair_index[:, 0:1] == slot_ids[None, :]).astype(jnp.float32)
    pick_second = (station_pair_index[:, 1:2] == slot_ids[None, :]).astype(jnp.float32)
    reliability_scale = (CELL_READINGS - rejected_cell_tally).astype(jnp.float32) / CELL_READINGS
    fetch_map = (my_fetch[:, None] == jnp.arange(station_list, dtype=jnp.int32)[None, :]).astype(
        jnp.float32
    )
    current = gain_values
    moment_one = first_moment
    moment_two = second_moment
    residual = jnp.zeros(measured_visibility.shape, jnp.float32)
    for iteration in range(ITERS):
        fetched = jnp.einsum(
            "ns,csx->cnx",
            fetch_map,
            lax.all_gather(current, "bl", axis=1, tiled=True),
            precision=HIGHEST,
        )
        gain_first = jnp.einsum("bn,cnx->cbx", pick_first, fetched, precision=HIGHEST)
        gain_second = jnp.einsum("bn,cnx->cbx", pick_second, fetched, precision=HIGHEST)
        residual, grad_first, grad_second = residual_terms(
            gain_first,
            gain_second,
            sky_model_visibility,
            measured_visibility,
            reliability_scale,
            spectral_blend_weight,
        )
        partial_value = jnp.einsum("bn,cbx->cnx", pick_first, grad_first, precision=HIGHEST)
        partial_value = partial_value + jnp.einsum(
            "bn,cbx->cnx", pick_second, grad_second, precision=HIGHEST
        )
        placed = jnp.einsum("ns,cnx->csx", fetch_map, partial_value, precision=HIGHEST)
        totals = lax.psum_scatter(placed, "bl", scatter_dimension=1, tiled=True)
        whole = lax.all_gather(totals, "ch", axis=2, tiled=True)
        kernel_rows = lax.dynamic_slice_in_dim(kernel, ch_index * chan_dev, chan_dev, 0)
        blended = jnp.einsum(
            "fg,csgk->csfk",
            kernel_rows,
            whole.reshape(2, own_count, -1, SKY_SOURCES),
            precision=HIGHEST,
        )
        smoothed = (1.0 - BLEND) * totals + BLEND * blended.reshape(2, own_count, width_dev)
        current, moment_one, moment_two = adam_update(
            current, moment_one, moment_two, smoothed, STEP + iteration + 1
        )
    return (current, moment_one, moment_two, residual)


def solution(mesh):
    placed = (
        P(None, "bl", "ch"),
        P(None, "bl", "ch"),
        P("bl", "ch"),
        P("bl", None),
        P(),
        P(None, "bl", "ch"),
        P(None, "bl", "ch"),
        P(None, "bl", "ch"),
    )
    return jax.shard_map(
        on_device,
        mesh=mesh,
        in_specs=placed,
        out_specs=(
            P(None, "bl", "ch"),
            P(None, "bl", "ch"),
            P(None, "bl", "ch"),
            P(None, "bl", "ch"),
        ),
        check_vma=False,
    )
```

profile of v0, /device:TPU:1, one launch (start us, length us, event | category | flops | bytes accessed | tf_op | source)
XLA Modules:
  0.0 1031.7 jit_solution(17458055501746909596)
XLA Ops:
  7.2 1.3 copy.104
  8.6 1.0 fusion.95
  10.1 0.8 slice_bitcast_fusion.1
  10.8 146.5 %all-gather.3.cloned.1.call-done = f32[2,512,512]{2,0,1:T(2,128)} async-done(((f32[2,4,512]{2,0,1:T(2,128)}), f32[2,512,512]{2,0,1:T(2,128)}) %all-gather.3.cloned.1.call-update) | async-done | bytes 2097168 | tf_op jit(solution)/shard_map/all_gather | solution.py:112
  157.3 2.7 fusion.6
  160.0 0.6 convolution_bitcast_fusion.4
  160.7 0.6 convolution_bitcast_fusion.5
  161.6 0.2 fusion.24
  161.8 0.4 fusion.12
  162.3 0.4 fusion.5
  162.7 1.1 convolution_bitcast_fusion.1
  163.8 2.4 copy.110
  166.3 1.3 dynamic-slice
  168.4 341.1 %all-reduce.5.cloned.1.call-done = f32[2,512,512]{2,0,1:T(2,128)} async-done(((f32[2,512,512]{2,0,1:T(2,128)}), f32[2,512,512]{2,0,1:T(2,128)}) %all-reduce.5.cloned.1.call-update) | async-done | bytes 2097168
  509.6 0.7 constant_dynamic-slice_fusion.1
  510.3 9.6 all_gather.13
  520.0 0.3 convolution_bitcast_fusion.7
  520.5 0.6 copy.114
  521.2 140.3 %all-gather.5.cloned.1.call-done = f32[2,512,512]{2,0,1:T(2,128)} async-done(((f32[2,4,512]{2,0,1:T(2,128)}), f32[2,512,512]{2,0,1:T(2,128)}) %all-gather.5.cloned.1.call-update) | async-done | bytes 2097168 | tf_op jit(solution)/shard_map/all_gather | solution.py:112
  661.5 2.7 fusion.9
  664.2 0.6 convolution_bitcast_fusion.3
  664.8 0.6 convolution_bitcast_fusion.2
  666.0 0.4 fusion.17
  666.4 0.4 fusion.4
  666.8 1.1 convolution_bitcast_fusion
  667.9 2.4 copy.118
  670.4 0.6 pad_maximum_fusion
  671.0 342.7 %all-reduce.7.cloned.1.call-done = f32[2,512,512]{2,0,1:T(2,128)} async-done(((f32[2,512,512]{2,0,1:T(2,128)}), f32[2,512,512]{2,0,1:T(2,128)}) %all-reduce.7.cloned.1.call-update) | async-done | bytes 2097168
  1013.7 0.7 constant_dynamic-slice_fusion
  1014.4 9.6 all_gather.15
  1024.2 0.3 convolution_bitcast_fusion.6
  1024.6 0.7 divide_subtract_fusion
  (42 shorter events, 2.2 us)
Async XLA Ops:
  7.2 2.7 copy-start
  7.2 150.2 %all-gather.3.cloned.1.call-start = ((), (), s32[]{:S(2)}) async-start(), calls=%async_computation | async-start | bytes 2113536 | tf_op jit(solution)/shard_map/all_gather | solution.py:112
  8.6 501.0 %all-reduce.5.cloned.1.call-start = ((), (), s32[]{:S(2)}) async-start(), calls=%async_computation.2 | async-start | bytes 4194304
  160.6 0.9 copy-start.1
  160.7 0.9 copy-start.5
  166.2 354.2 %copy-start.2 = (f32[2,4,512]{2,1,0:T(4,128)S(1)}, f32[2,4,512]{2,1,0:T(4,128)}, u32[]{:S(2)}) copy-start(f32[2,4,512]{2,1,0:T(4,128)} %param.14) | copy-start | bytes 49156
  166.2 354.2 %copy-start.3 = (f32[2,4,512]{2,1,0:T(4,128)S(1)}, f32[2,4,512]{2,1,0:T(4,128)}, u32[]{:S(2)}) copy-start(f32[2,4,512]{2,1,0:T(4,128)} %param.15) | copy-start | bytes 49156
  166.2 354.2 %copy-start.4 = (f32[2,4,512]{2,1,0:T(4,128)S(1)}, f32[2,4,512]{2,1,0:T(4,128)}, u32[]{:S(2)}) copy-start(f32[2,4,512]{2,1,0:T(4,128)} %param.13) | copy-start | bytes 49156
  166.2 495.3 %all-gather.5.cloned.1.call-start = ((), (), s32[]{:S(2)}) async-start(), calls=%async_computation.1 | async-start | bytes 2113536 | tf_op jit(solution)/shard_map/all_gather | solution.py:112
  521.1 492.6 %all-reduce.7.cloned.1.call-start = ((), (), s32[]{:S(2)}) async-start(), calls=%async_computation.3 | async-start | bytes 4194304
Sparse Core Ops, SparseCore 0:
  11.7 145.5 all-gather.2
  166.4 343.1 all-reduce.4
  521.3 140.2 all-gather.4
  670.5 343.1 all-reduce.6
where the time goes:
time: 1030 us
  waiting for transfers between devices  971 us (94%)
  blocking collectives  19.2 us (2%)
  between operations  14.7 us (1%)
  local copies, waits for them, and re-layouts  12.3 us (1%)
  matrix products  12.3 us (1%)
    unnamed x6, waiting for transfers between devices  684 us
    all_gather x2, waiting for transfers between devices, on_device(): lax.all_gather(current, 'bl', axis=1, tiled=True)  287 us
  transfers between devices with their start and end apart: 4, of which 4 were waited for; matrix products, arithmetic and copies ran while one was open for 0% of the time, Pallas kernels for 0%

commit v1 on v0

v1 whole, which is shorter than its diff:
```python
import math

import jax
import jax.numpy as jnp
from jax import lax
from jax.experimental import pallas as pl
from jax.experimental.pallas import tpu as pltpu
from jax.sharding import PartitionSpec as P

MESH = pl.DeviceIdType.MESH
F32, BF16, I32 = jnp.float32, jnp.bfloat16, jnp.int32

SKY_SOURCES = 32
CELL_READINGS = 16
ITERS = 2
STEP = 3
BETA_ONE = 0.9
BETA_TWO = 0.99
ADAM_EPSILON = 1e-08
LEARN_RATE = 0.3
BLEND = 0.5

NX, NY, NZ, NS = 4, 4, 16, 8
NCHAN = 64
FAR = 5
CENTRES = (-FAR, 0, FAR)
STEPS = (1, -1, 2, -2)
ORDER = [j for j in CENTRES] + [j - n for n in STEPS for j in CENTRES] + [8]
SLOT = {rel % NZ: slot for slot, rel in enumerate(ORDER)}
NEAR_ROWS = 32 * len(CENTRES)
ROWS = 32 * NZ
PLANE = ((2, 0), (2, 1), (1, 0), (3, 0), (1, 1), (3, 1), (0, 1))
NBL = 128
CROWS = 136
DECAY = 2.0 / NCHAN


def remote(src, dst, send_sem, recv_sem, device):
    return pltpu.make_async_remote_copy(
        src_ref=src, dst_ref=dst, send_sem=send_sem, recv_sem=recv_sem, device_id=device, device_id_type=MESH
    )


def kernel(
    c_ref, meas_ref, rej_ref, pair_ref, fetch_ref, g_ref, m_ref, v_ref,
    go_ref, mo_ref, vo_ref, res_ref,
    csend, crecv, misc, pick, gsplit, grads, state_g, state_m, state_v,
    gpiece, zg, zp, rsn, rsh, accp, rsp, tots, xs, xr, ressend, resrecv, resmat,
    c_ss, c_rs, a1_ss, a1_rs, a2_ss, a2_rs, ah_ss, ah_rs, r1_ss, r1_rs, rh_ss, rh_rs, r2_ss, r2_rs, x_ss, x_rs, o_ss, o_rs,
):
    bl, x = lax.axis_index("bl"), lax.axis_index("ch")
    y, z, c = lax.div(bl, 2 * NZ), lax.rem(lax.div(bl, 2), NZ), lax.rem(bl, 2)
    s = 2 * y + c

    def device(s_to, dz=0, dx=0):
        z_to, x_to = lax.rem(z + dz + NZ, NZ), lax.rem(x + dx, NX)
        return ((lax.div(s_to, 2) * NZ + z_to) * 2 + lax.rem(s_to, 2), x_to)

    def mate(dy, dc):
        return 2 * lax.rem(y + dy, NY) + lax.rem(c + dc, 2)

    mates = [mate(dy, dc) for dy, dc in PLANE]

    barrier = pltpu.get_barrier_semaphore()
    partners = [device(s, j) if k == NS - 1 else device(mates[k], j) for j in CENTRES for k in range(NS) if j or k < NS - 1]
    partners += [device(s, n) for n in (1, -1, 2, -2, 3, -3)] + [device(s, 0, dx) for dx in (1, 2, 3)]
    for partner in partners:
        pl.semaphore_signal(barrier, inc=1, device_id=partner, device_id_type=MESH)

    lane8 = lax.broadcasted_iota(I32, (8, 128), 1)
    low8 = lane8 < 64

    def to_pieces(ref, out):
        for t in range(4):
            both = jnp.concatenate([ref[0, :, 128 * t : 128 * t + 128], ref[1, :, 128 * t : 128 * t + 128]], axis=0)
            turned = pltpu.roll(both, 64, 1)
            left = jnp.concatenate([both[0:4], turned[0:4]], axis=0)
            right = jnp.concatenate([turned[4:8], both[4:8]], axis=0)
            out[8 * t : 8 * t + 8, :] = jnp.where(low8, left, right)

    def from_pieces(value, ref):
        for t in range(4):
            both = value[8 * t : 8 * t + 8]
            turned = pltpu.roll(both, 64, 1)
            left = jnp.concatenate([both[0:4], turned[0:4]], axis=0)
            right = jnp.concatenate([turned[4:8], both[4:8]], axis=0)
            mixed = jnp.where(low8, left, right)
            ref[0, :, 128 * t : 128 * t + 128] = mixed[0:4]
            ref[1, :, 128 * t : 128 * t + 128] = mixed[4:8]

    to_pieces(g_ref, state_g)
    for k in range(NS):
        gpiece[0, k] = state_g[4 * k : 4 * k + 4, :]

    misc[:, 0:16] = meas_ref[0]
    misc[:, 16:32] = meas_ref[1]
    misc[:, 32:48] = (CELL_READINGS - rej_ref[...]).astype(F32) / CELL_READINGS
    fetch_row = fetch_ref[pl.ds(bl, 1), :].astype(F32)
    places = lax.broadcasted_iota(I32, (NBL, fetch_ref.shape[1]), 1)
    for i in range(2):
        station = jnp.where(pair_ref[:, i : i + 1] == places, fetch_row, 0.0)
        misc[:, 48 + i : 49 + i] = jnp.sum(station, axis=1, keepdims=True)
    turned = misc[...].T
    station = turned[48:50].astype(I32)
    rel = ((station >> 3) & (NZ - 1)) - z
    rel = jnp.where(rel < 0, rel + NZ, rel)
    slot = jnp.zeros_like(rel)
    for k in range(NZ):
        slot = jnp.where(rel == k, SLOT[k], slot)
    rows = (slot * 32 + (station >> 7) * 8 + (station & 7)).astype(F32)
    for t in range(4):
        for ri in range(2):
            block = c_ref[ri, :, 128 * t : 128 * t + 128].astype(F32).T
            csend[2 * t, 64 * ri : 64 * ri + 64] = block[0:64]
            csend[2 * t + 1, 64 * ri : 64 * ri + 64] = block[64:128]
    for k in range(NS):
        for i in range(3):
            csend[k, 128 + 2 * i : 130 + 2 * i] = turned[16 * i + 2 * k : 16 * i + 2 * k + 2]
        csend[k, 134:136] = rows

    pl.semaphore_wait(barrier, len(partners))

    def gains_copy(it, j, k):
        to = s if k is None else mates[k]
        return remote(
            gpiece.at[it, to], zg.at[it, 2 - j, s], a1_ss.at[it, j, to], a1_rs.at[it, 2 - j, s], device(to, CENTRES[j])
        )

    def gains_out(it):
        sent = []
        for j in (0, 2, 1):
            for k in [*range(NS - 1)] + ([None] if j != 1 else []):
                copy = gains_copy(it, j, k)
                copy.start()
                sent.append(copy)
        return sent

    def gains_on(it):
        sent = []
        zg[it, 1, s] = gpiece[it, s]
        for j in (1, 0, 2):
            for k in [*range(NS - 1)] + ([None] if j != 1 else []):
                source = s if k is None else mates[k]
                remote(
                    gpiece.at[it, s], zg.at[it, j, source], a1_ss.at[it, j, s], a1_rs.at[it, j, source], device(mates[0])
                ).wait_recv()
            for i, n in enumerate(STEPS):
                slot = 3 * (i + 1) + j
                copy = remote(zg.at[it, j], zg.at[it, slot], a2_ss.at[it, i, j], a2_rs.at[it, i, j], device(s, n))
                copy.start()
                sent.append(copy)
            if j != 1:
                half = pl.ds(2 * j, 4)
                copy = remote(
                    zg.at[it, j, half], zg.at[it, 15, half], ah_ss.at[it, j], ah_rs.at[it, j], device(s, 3 if j == 0 else -3)
                )
                copy.start()
                sent.append(copy)
        return sent

    def drain(copies):
        for copy in copies:
            copy.wait_send()

    sent_gains = gains_out(0)
    sent_c = []
    for k in range(NS - 1):
        copy = remote(csend.at[mates[k]], crecv.at[s], c_ss.at[mates[k]], c_rs.at[s], device(mates[k]))
        copy.start()
        sent_c.append(copy)
    crecv[s] = csend[s]
    to_pieces(m_ref, state_m)
    to_pieces(v_ref, state_v)
    sent_on = gains_on(0)

    def source_of(i):
        half = lax.div(i, 2)
        dy = jnp.where(half == 2, 3, jnp.where(half == 3, 2, half))
        return 2 * lax.rem(y + dy, NY) + lax.rem(c + i, 2)

    row_id = lax.broadcasted_iota(I32, (ROWS, NBL), 0)

    def picks(i, source):
        for k in range(2):
            row = crecv[source, 134 + k : 135 + k, :].astype(I32)
            where = pl.multiple_of(256 * i + 128 * k, 128)
            pick[:, pl.ds(where, 128)] = jnp.where(row_id == row, 1.0, 0.0).astype(BF16)

    picks(0, s)

    def next_picks(i, carry):
        source = source_of(i)
        remote(csend.at[0], crecv.at[source], c_ss.at[s], c_rs.at[source], device(mates[0])).wait_recv()
        picks(i, source)
        return carry

    lax.fori_loop(1, NS, next_picks, 0)

    lane32 = lax.broadcasted_iota(I32, (32, 128), 1)
    odd32 = (lane32 & 32) != 0
    odd8 = (lane8 & 32) != 0
    pair32 = lax.broadcasted_iota(I32, (32, 128), 0) >> 2
    chan = 2 * pair32 + jnp.where(odd32, 1, 0)
    a1 = math.exp(-DECAY)

    def decay(steps):
        return jnp.exp(-DECAY * steps.astype(F32))

    whole_chan = chan + 16 * x
    geometric = 1.0 / (1.0 - a1)
    norm = (1.0 - decay(whole_chan + 1)) * geometric + (a1 - decay(NCHAN - whole_chan)) * geometric
    half_norm = BLEND / norm
    from_left = decay(chan + 1)
    from_right = decay(16 - chan)
    near_left = jnp.where(odd32, a1 * a1, a1)
    near_right = jnp.where(odd32, a1, a1 * a1)
    up = jnp.where(odd32, 1.0, a1)
    down = jnp.where(odd32, a1, 1.0)

    def swap(value):
        return jnp.where((lax.broadcasted_iota(I32, value.shape, 1) & 32) != 0, pltpu.roll(value, 32, 1), pltpu.roll(value, 96, 1))

    def smooth(it):
        total = tots[...]
        swapped = swap(total)
        right_going = total * up + swapped * down
        left_going = total * down + swapped * up
        blended = total + a1 * swapped
        zero = jnp.zeros((4, 128), F32)
        lefts, rights = [zero], [zero]
        for k in range(NS):
            lefts.append(a1 * a1 * lefts[-1] + right_going[4 * k : 4 * k + 4])
            q = NS - 1 - k
            rights.append(a1 * a1 * rights[-1] + left_going[4 * q : 4 * q + 4])
        out8 = jnp.concatenate([jnp.where(odd8[0:4], rights[NS], lefts[NS])] * 2, axis=0)
        xs[it] = out8[0:4]
        sent = []
        for dx in (2, 1, 3):
            copy = remote(xs.at[it], xr.at[it, dx - 1], x_ss.at[it, dx - 1], x_rs.at[it, dx - 1], device(s, 0, dx))
            copy.start()
            sent.append(copy)
        left_all = jnp.concatenate(lefts[:NS], axis=0)
        right_all = jnp.concatenate(rights[NS - 1 :: -1], axis=0)
        blended = blended + near_left * left_all + near_right * right_all
        across = jnp.zeros((4, 128), F32)
        weights = []
        for dx in (1, 2, 3):
            source = lax.rem(x - dx + NX, NX)
            gap = jnp.full((8, 128), jnp.abs(x - source), I32)
            is_left = jnp.full((8, 128), x - source, I32) > 0
            used = jnp.where(is_left, jnp.where(odd8, 0, 1), jnp.where(odd8, 1, 0)).astype(F32)
            weights.append((used * decay(16 * (gap - 1)))[0:4])
        for dx in (1, 2, 3):
            remote(xs.at[it], xr.at[it, dx - 1], x_ss.at[it, dx - 1], x_rs.at[it, dx - 1], device(s, 0, dx)).wait_recv()
        for dx in (1, 2, 3):
            across = across + xr[it, dx - 1] * weights[dx - 1]
        across = jnp.concatenate([across] * 8, axis=0)
        other = swap(across)
        blended = blended + from_left * jnp.where(odd32, other, across) + from_right * jnp.where(odd32, across, other)
        return (1.0 - BLEND) * total + half_norm * blended, sent

    coef = -2.0 / math.sqrt(2.0 * NBL * NS * NZ / (4 * NS * NZ))

    for it in range(ITERS):
        last = it == ITERS - 1
        for j in (0, 1, 2):
            for i in range(len(STEPS)):
                slot = 3 * (i + 1) + j
                remote(
                    zg.at[it, j], zg.at[it, slot], a2_ss.at[it, i, j], a2_rs.at[it, i, j], device(s, STEPS[i])
                ).wait_recv()
        for j in (0, 2):
            half = pl.ds(2 * j, 4)
            remote(zg.at[it, j, half], zg.at[it, 15, half], ah_ss.at[it, j], ah_rs.at[it, j], device(s, 3)).wait_recv()
        for t in range(4):
            block = zg[it, 4 * t : 4 * t + 4].reshape(128, 128).T
            high = block.astype(BF16)
            gsplit[0:128, 128 * t : 128 * t + 128] = high
            gsplit[128:256, 128 * t : 128 * t + 128] = (block - high.astype(F32)).astype(BF16)

        def chunk(i, carry, last=last):
            source = source_of(i)
            at = pl.multiple_of(256 * i, 256)
            both = jnp.dot(gsplit[...], pick[:, pl.ds(at, 256)], preferred_element_type=F32)
            both = both[0:128] + both[128:256]
            ga, gb = both[0:64, 0:128], both[64:128, 0:128]
            gc, gd = both[0:64, 128:256], both[64:128, 128:256]
            cr, ci = crecv[source, 0:64, :], crecv[source, 64:128, :]
            u = ga * gc + gb * gd
            v = gb * gc - ga * gd
            model_re = jnp.sum((u * cr - v * ci).reshape(2, SKY_SOURCES, NBL), axis=1)
            model_im = jnp.sum((u * ci + v * cr).reshape(2, SKY_SOURCES, NBL), axis=1)
            weight = crecv[source, 132:134, :]
            err_re = weight * (crecv[source, 128:130, :] - model_re)
            err_im = weight * (crecv[source, 130:132, :] - model_im)
            if last:
                ressend[source] = jnp.concatenate([err_re, err_im], axis=0)
            wide = (2, SKY_SOURCES, NBL)
            sr = jnp.broadcast_to((coef * err_re)[:, None, :], wide).reshape(64, NBL)
            si = jnp.broadcast_to((coef * err_im)[:, None, :], wide).reshape(64, NBL)
            px = gc * cr + gd * ci
            py = gd * cr - gc * ci
            qx = ga * cr - gb * ci
            qy = ga * ci + gb * cr
            terms = ((sr * px - si * py, sr * py + si * px), (sr * qx + si * qy, sr * qy - si * qx))
            for k in range(2):
                for ri in range(2):
                    value = terms[k][ri]
                    high = value.astype(BF16)
                    where = pl.ds(pl.multiple_of(256 * i + 128 * k, 128), 128)
                    grads[64 * ri : 64 * ri + 64, where] = high
                    grads[128 + 64 * ri : 192 + 64 * ri, where] = (value - high.astype(F32)).astype(BF16)
            return carry

        lax.fori_loop(0, NS, chunk, 0)

        both = lax.dot_general(pick[...], grads[...], (((1,), (1,)), ((), ())), preferred_element_type=F32)
        zp[it] = both[:, 0:128] + both[:, 128:256]
        sent_near = []
        for i, n in enumerate(STEPS):
            copy = remote(
                zp.at[it, pl.ds(NEAR_ROWS * (i + 1), NEAR_ROWS)], rsn.at[it, i], r1_ss.at[it, i], r1_rs.at[it, i], device(s, -n)
            )
            copy.start()
            sent_near.append(copy)
        for h in range(2):
            copy = remote(
                zp.at[it, pl.ds(480 + 16 * h, 16)], rsh.at[it, h], rh_ss.at[it, h], rh_rs.at[it, h], device(s, 6 * h - 3)
            )
            copy.start()
            sent_near.append(copy)
        sent_res = []
        if last:
            for k in range(NS - 1):
                copy = remote(ressend.at[mates[k]], resrecv.at[s], o_ss.at[mates[k]], o_rs.at[s], device(mates[k]))
                copy.start()
                sent_res.append(copy)
            resrecv[s] = ressend[s]
        else:
            drain(sent_c)
        drain(sent_gains)
        drain(sent_on)
        for copy in sent_near:
            copy.wait_recv()
        acc = zp[it, 0:NEAR_ROWS, :]
        for i in range(len(STEPS)):
            acc = acc + rsn[it, i]
        parts = [acc[0:16] + rsh[it, 0], acc[16:32], acc[32:64], acc[64:80], acc[80:96] + rsh[it, 1]]
        acc = jnp.concatenate(parts, axis=0)
        for j in range(3):
            for k in range(NS):
                accp[it, j, k] = acc[32 * j + 4 * k : 32 * j + 4 * k + 4]
        sent_far = []
        for j in (0, 2, 1):
            for k in [*range(NS - 1)] + ([None] if j != 1 else []):
                to = s if k is None else mates[k]
                copy = remote(
                    accp.at[it, j, to], rsp.at[it, j, s], r2_ss.at[it, j, to], r2_rs.at[it, j, s], device(to, CENTRES[j])
                )
                copy.start()
                sent_far.append(copy)
        rsp[it, 1, s] = accp[it, 1, s]
        drain(sent_near)
        if last:
            drain(sent_res)
            for k in range(NS - 1):
                remote(
                    ressend.at[s], resrecv.at[mates[k]], o_ss.at[s], o_rs.at[mates[k]], device(mates[k])
                ).wait_recv()
            for k in range(NS):
                for ri in range(2):
                    resmat[16 * ri + 2 * k : 16 * ri + 2 * k + 2, :] = resrecv[k, 2 * ri : 2 * ri + 2, :]
            final = resmat[...].T
            res_ref[0] = final[:, 0:16]
            res_ref[1] = final[:, 16:32]
        for j in (1, 0, 2):
            for k in [*range(NS - 1)] + ([None] if j != 1 else []):
                source = s if k is None else mates[k]
                remote(
                    accp.at[it, j, s], rsp.at[it, j, source], r2_ss.at[it, j, s], r2_rs.at[it, j, source], device(mates[0])
                ).wait_recv()
        for k in range(NS):
            tots[4 * k : 4 * k + 4, :] = rsp[it, 0, k] + rsp[it, 1, k] + rsp[it, 2, k]

        smoothed, sent_x = smooth(it)
        tally = STEP + it + 1
        new_m = BETA_ONE * state_m[...] + (1.0 - BETA_ONE) * smoothed
        new_v = BETA_TWO * state_v[...] + (1.0 - BETA_TWO) * smoothed * smoothed
        first_hat = new_m / (1.0 - BETA_ONE**tally)
        second_hat = new_v / (1.0 - BETA_TWO**tally)
        new_g = state_g[...] - LEARN_RATE * first_hat / (jnp.sqrt(second_hat) + ADAM_EPSILON)
        if last:
            from_pieces(new_g, go_ref)
            from_pieces(new_m, mo_ref)
            from_pieces(new_v, vo_ref)
            drain(sent_far)
            drain(sent_x)
        else:
            for k in range(NS):
                gpiece[it + 1, k] = new_g[4 * k : 4 * k + 4]
            sent_gains = gains_out(it + 1)
            state_g[...] = new_g
            state_m[...] = new_m
            state_v[...] = new_v
            drain(sent_far)
            drain(sent_x)
            sent_on = gains_on(it + 1)


def on_device(*args):
    coherency, measured = args[0], args[1]
    gains = args[5]
    out = [jax.ShapeDtypeStruct(gains.shape, F32)] * 3 + [jax.ShapeDtypeStruct(measured.shape, F32)]
    vmem = pl.BlockSpec(memory_space=pltpu.VMEM)
    sem = pltpu.SemaphoreType.DMA
    buf = pltpu.VMEM
    return pl.pallas_call(
        kernel,
        out_shape=out,
        in_specs=[vmem] * 8,
        out_specs=[vmem] * 4,
        scratch_shapes=[
            buf((NS, CROWS, NBL), F32),
            buf((NS, CROWS, NBL), F32),
            buf((NBL, 128), F32),
            buf((ROWS, 2 * NBL * NS), BF16),
            buf((256, ROWS), BF16),
            buf((256, 2 * NBL * NS), BF16),
            buf((32, 128), F32),
            buf((32, 128), F32),
            buf((32, 128), F32),
            buf((ITERS, NS, 4, 128), F32),
            buf((ITERS, NZ, NS, 4, 128), F32),
            buf((ITERS, ROWS, 128), F32),
            buf((ITERS, 4, NEAR_ROWS, 128), F32),
            buf((ITERS, 2, 16, 128), F32),
            buf((ITERS, 3, NS, 4, 128), F32),
            buf((ITERS, 3, NS, 4, 128), F32),
            buf((32, 128), F32),
            buf((ITERS, 4, 128), F32),
            buf((ITERS, 3, 4, 128), F32),
            buf((NS, 4, 128), F32),
            buf((NS, 4, 128), F32),
            buf((128, 128), F32),
            sem((NS,)), sem((NS,)),
            sem((ITERS, 3, NS)), sem((ITERS, 3, NS)),
            sem((ITERS, 4, 3)), sem((ITERS, 4, 3)),
            sem((ITERS, 3)), sem((ITERS, 3)),
            sem((ITERS, 4)), sem((ITERS, 4)),
            sem((ITERS, 2)), sem((ITERS, 2)),
            sem((ITERS, 3, NS)), sem((ITERS, 3, NS)),
            sem((ITERS, 3)), sem((ITERS, 3)),
            sem((NS,)), sem((NS,)),
        ],
        compiler_params=pltpu.CompilerParams(collective_id=0, has_side_effects=True, vmem_limit_bytes=40 * 2**20),
        cost_estimate=pl.CostEstimate(flops=4 * 10**9, bytes_accessed=2**20, transcendentals=10**4),
        name="calibrate",
    )(*args)


def solution(mesh):
    split = P(None, "bl", "ch")
    return jax.shard_map(
        on_device,
        mesh=mesh,
        in_specs=(split, split, P("bl", "ch"), P("bl", None), P(), split, split, split),
        out_specs=(split,) * 4,
        check_vma=False,
    )
```

time: 1030 us -> 90.7 us (0.09)
  waiting for transfers between devices: 971 us -> 0 us
  Pallas kernels: 0 us -> 84.6 us
  blocking collectives: 19.2 us -> 0 us
  between operations: 14.7 us -> 0.72 us
  matrix products: 12.3 us -> 0 us
    unnamed x6 -> x0, waiting for transfers between devices: 684 us -> none
    all_gather x2 -> x0, waiting for transfers between devices: 287 us -> none  [on_device(): lax.all_gather(current, 'bl', axis=1, tiled=True)]
    pallas_call x0 -> x1, Pallas kernels: none -> 84.6 us  [on_device(): pl.pallas_call(kernel, out_shape=out, in_specs=[vmem] * 8, out_specs=[vme...]
    all_gather x2 -> x0, blocking collectives: 19.2 us -> none  [on_device(): whole = lax.all_gather(totals, 'ch', axis=2, tiled=True)]
    dot_general x14 -> x0, matrix products: 12.3 us -> none  [the longest x2 5.39 us: on_device(): jnp.einsum('ns,csx->cnx', fetch_map, lax.all_gather(current, 'bl', axis=1...]
  transfers between devices with their start and end apart: 4 -> 0, of which waited for: 4 -> 0; matrix products, arithmetic and copies ran while one was open for 0% -> 0% of each run, Pallas kernels for 0% -> 0%
where the time goes in v1:
time: 90.7 us; the launch traced here: 90.4 us
  Pallas kernels  84.6 us (93%)
  local copies, waits for them, and re-layouts  5.15 us (6%)
    pallas_call x1, Pallas kernels, on_device(): pl.pallas_call(kernel, out_shape=out, in_specs=[vmem] * 8, out_specs=[vme...  84.6 us
    unnamed x17, local copies, waits for them, and re-layouts  4.47 us

profile of v1, /device:TPU:1, one launch (start us, length us, event | category | flops | bytes accessed | tf_op | source)
XLA Modules:
  0.0 90.4 jit_solution(12722208194805786368)
XLA Ops:
  0.6 0.0 copy-start.4
  0.6 0.0 copy-start
  0.7 0.8 copy.13.rej_ref
  1.5 0.0 copy-done.4
  1.5 0.1 copy.14.pair_ref
  1.6 0.8 copy.15.fetch_ref
  2.5 0.0 copy-start.1
  2.5 0.0 copy-start.2
  2.5 0.0 copy-start.3
  2.5 0.8 copy.12.meas_ref
  3.3 0.0 copy-done
  3.3 0.0 copy-done.1
  3.3 0.0 copy-done.2
  3.4 0.0 copy-done.3
  3.4 84.6 %calibrate.1 = (f32[2,4,512]{2,1,0:T(4,128)S(1)}, f32[2,4,512]{2,1,0:T(4,128)S(1)}, f32[2,4,512]{2,1,0:T(4,128)S(1)}, f32[2,128,16]{2,1,0:T(8,128)S(1)}) custom-call(bf16[2,128,512]{2,1,0:T(8,128)(2,1)S(1)} %copy-done, f32[2,128,16]{2,1,0:T(8,128)S(1)} %copy.12.meas_ref, s32[128,16]{1,0:T(8,128)S(1)} %copy.13.rej_ref, s32[128,2]{1,0:T(8,128)S(1)} %copy.14.pair_ref, ...), custom_call_target="tpu_custom_call" | custom-call | flops 4000000000 | bytes 1048576 | tf_op jit(solution)/shard_map/calibrate/pallas_call | solution.py:417
  87.9 0.7 copy.16
  88.6 0.6 copy.20
  89.2 0.6 copy.21
  89.8 0.6 copy.22
Async XLA Ops:
  0.6 0.9 copy-start.4
  0.6 2.7 %copy-start = (bf16[2,128,512]{2,1,0:T(8,128)(2,1)S(1)}, bf16[2,128,512]{2,1,0:T(8,128)(2,1)}, u32[]{:S(2)}) copy-start(bf16[2,128,512]{2,1,0:T(8,128)(2,1)} %c_ref.1) | copy-start | bytes 786436
  2.5 0.9 copy-start.1
  2.5 0.9 copy-start.2
  2.5 0.9 copy-start.3

commit v2 on v1

v2 whole, which is shorter than its diff:
```python
import math

import jax
import jax.numpy as jnp
from jax import lax
from jax.experimental import pallas as pl
from jax.experimental.pallas import tpu as pltpu
from jax.sharding import PartitionSpec as P

MESH = pl.DeviceIdType.MESH
F32, BF16, I32 = jnp.float32, jnp.bfloat16, jnp.int32

SKY_SOURCES = 32
CELL_READINGS = 16
ITERS = 2
STEP = 3
BETA_ONE = 0.9
BETA_TWO = 0.99
ADAM_EPSILON = 1e-08
LEARN_RATE = 0.3
BLEND = 0.5

NX, NY, NZ, NS = 4, 4, 16, 8
NCHAN = 64
FAR = 5
CENTRES = (-FAR, FAR, 0)
STEPS = (1, -1, 2, -2)
ORDER = [-FAR, FAR] + [j - n for n in STEPS for j in (-FAR, FAR)] + [8] + [0] + [-n for n in STEPS]
SLOT = {rel % NZ: slot for slot, rel in enumerate(ORDER)}
OPPOSITE, OWN = 10, 11
HOME = (0, 1, OWN)
BACK = (1, 0, OWN)
ROWS = 32 * NZ
PLANE = ((2, 0), (2, 1), (1, 0), (3, 0), (1, 1), (3, 1), (0, 1))
NBL = 128
CROWS = 136
DECAY = 2.0 / NCHAN


def remote(src, dst, send_sem, recv_sem, device):
    return pltpu.make_async_remote_copy(
        src_ref=src, dst_ref=dst, send_sem=send_sem, recv_sem=recv_sem, device_id=device, device_id_type=MESH
    )


def kernel(
    c_hbm, meas_hbm, rej_hbm, pair_hbm, fetch_hbm, g_hbm, m_hbm, v_hbm,
    go_ref, mo_ref, vo_ref, res_ref,
    c_ref, meas_ref, rej_ref, pair_ref, fetch_ref, g_ref, m_ref, v_ref, in_sem,
    csend, crecv, pick, gsplit, grads, state_g, state_m, state_v,
    gpiece, zg, zp, rsn, rsc, rsh, accp, rsp, tots, xs, xr, ressend, resrecv,
    c_ss, c_rs, a1_ss, a1_rs, a2_ss, a2_rs, r1_ss, r1_rs, rc_ss, rc_rs, rh_ss, rh_rs, r2_ss, r2_rs, x_ss, x_rs, o_ss, o_rs,
):
    bl, x = lax.axis_index("bl"), lax.axis_index("ch")
    y, z, c = lax.div(bl, 2 * NZ), lax.rem(lax.div(bl, 2), NZ), lax.rem(bl, 2)
    s = 2 * y + c

    def device(s_to, dz=0, dx=0):
        z_to, x_to = lax.rem(z + dz + NZ, NZ), lax.rem(x + dx, NX)
        return ((lax.div(s_to, 2) * NZ + z_to) * 2 + lax.rem(s_to, 2), x_to)

    def mate(dy, dc):
        return 2 * lax.rem(y + dy, NY) + lax.rem(c + dc, 2)

    mates = [mate(dy, dc) for dy, dc in PLANE]

    barrier = pltpu.get_barrier_semaphore()
    partners = [device(s, j) if k == NS - 1 else device(mates[k], j) for j in CENTRES for k in range(NS) if j or k < NS - 1]
    partners += [device(s, n) for n in (1, -1, 2, -2, 3, -3)] + [device(s, 0, dx) for dx in (1, 2, 3)]
    for partner in partners:
        pl.semaphore_signal(barrier, inc=1, device_id=partner, device_id_type=MESH)

    loads = [
        pltpu.make_async_copy(src, dst, in_sem.at[i])
        for i, (src, dst) in enumerate(
            [
                (g_hbm, g_ref), (pair_hbm, pair_ref), (fetch_hbm, fetch_ref), (rej_hbm, rej_ref), (meas_hbm, meas_ref),
                (c_hbm, c_ref), (m_hbm, m_ref), (v_hbm, v_ref),
            ]
        )
    ]
    for load in loads:
        load.start()
    lane8 = lax.broadcasted_iota(I32, (8, 128), 1)
    low8 = lane8 < 64

    def to_pieces(ref, out):
        for t in range(4):
            both = jnp.concatenate([ref[0, :, 128 * t : 128 * t + 128], ref[1, :, 128 * t : 128 * t + 128]], axis=0)
            turned = pltpu.roll(both, 64, 1)
            left = jnp.concatenate([both[0:4], turned[0:4]], axis=0)
            right = jnp.concatenate([turned[4:8], both[4:8]], axis=0)
            out[8 * t : 8 * t + 8, :] = jnp.where(low8, left, right)

    def from_pieces(value, ref):
        for t in range(4):
            both = value[8 * t : 8 * t + 8]
            turned = pltpu.roll(both, 64, 1)
            left = jnp.concatenate([both[0:4], turned[0:4]], axis=0)
            right = jnp.concatenate([turned[4:8], both[4:8]], axis=0)
            mixed = jnp.where(low8, left, right)
            ref[0, :, 128 * t : 128 * t + 128] = mixed[0:4]
            ref[1, :, 128 * t : 128 * t + 128] = mixed[4:8]

    loads[0].wait()
    to_pieces(g_ref, state_g)
    for k in range(NS):
        gpiece[0, k] = state_g[4 * k : 4 * k + 4, :]

    for load in loads[1:5]:
        load.wait()
    fetch = jnp.where(lax.broadcasted_iota(I32, fetch_ref.shape, 1) == bl, fetch_ref[...], 0).astype(F32)
    fetch = jnp.sum(fetch, axis=1, keepdims=True)
    places = lax.broadcasted_iota(I32, (fetch_ref.shape[0], NBL), 0)
    station = jnp.concatenate(
        [
            jnp.sum(jnp.where(places == pair_ref[i : i + 1, :], fetch, 0.0), axis=0, keepdims=True)
            for i in range(2)
        ],
        axis=0,
    ).astype(I32)
    rel = ((station >> 3) & (NZ - 1)) - z
    rel = jnp.where(rel < 0, rel + NZ, rel)
    slot = jnp.zeros_like(rel)
    for k in range(NZ):
        slot = jnp.where(rel == k, SLOT[k], slot)
    weights = (CELL_READINGS - rej_ref[...]).astype(F32) / CELL_READINGS
    rows = (slot * 32 + (station >> 7) * 8 + (station & 7)).astype(F32)
    loads[5].wait()
    for t in range(4):
        for ri in range(2):
            block = c_ref[ri, :, 128 * t : 128 * t + 128].astype(F32).T
            csend[2 * t, 64 * ri : 64 * ri + 64] = block[0:64]
            csend[2 * t + 1, 64 * ri : 64 * ri + 64] = block[64:128]
    for k in range(NS):
        for ri in range(2):
            csend[k, 128 + 2 * ri : 130 + 2 * ri] = meas_ref[ri, 2 * k : 2 * k + 2, :]
        csend[k, 132:134] = weights[2 * k : 2 * k + 2]
        csend[k, 134:136] = rows

    pl.semaphore_wait(barrier, len(partners))

    def waiter(ref, send_sem, recv_sem):
        return remote(ref, ref, send_sem, recv_sem, device(mates[0]))

    def gains_out(it):
        for j in range(3):
            for k in [*range(NS - 1)] + ([None] if j != 2 else []):
                to = s if k is None else mates[k]
                remote(
                    gpiece.at[it, to], zg.at[it, BACK[j], s], a1_ss.at[it], a1_rs.at[it, (1, 0, 2)[j]], device(to, CENTRES[j])
                ).start()

    def gains_on(it):
        def near_copy(i, own):
            width = 1 if own else 2
            src, dst = (OWN, OWN + 1 + i) if own else (0, 2 + 2 * i)
            return remote(
                zg.at[it, pl.ds(src, width)], zg.at[it, pl.ds(dst, width)], a2_ss.at[it], a2_rs.at[it, own], device(s, STEPS[i])
            )

        def half_copy(h):
            half = pl.ds(4 * h, 4)
            return remote(
                zg.at[it, h, half], zg.at[it, OPPOSITE, half], a2_ss.at[it], a2_rs.at[it, 0], device(s, 3 - 6 * h)
            )

        zg[it, OWN, s] = gpiece[it, s]
        waiter(zg.at[it, OWN, pl.ds(0, NS - 1)], a1_ss.at[it], a1_rs.at[it, 2]).wait_recv()
        for i in range(len(STEPS)):
            near_copy(i, 1).start()
        for h in range(2):
            waiter(zg.at[it, h], a1_ss.at[it], a1_rs.at[it, h]).wait_recv()
            half_copy(h).start()
        for i in range(len(STEPS)):
            near_copy(i, 0).start()

    def gains_in(it):
        waiter(zg.at[it, pl.ds(OWN + 1, 4)], a2_ss.at[it], a2_rs.at[it, 1]).wait_recv()
        waiter(zg.at[it, pl.ds(2, 9)], a2_ss.at[it], a2_rs.at[it, 0]).wait_recv()

    def gains_sent(it):
        waiter(zg.at[it, pl.ds(0, 2)], a1_ss.at[it], a1_rs.at[it, 0]).wait_send()
        waiter(zg.at[it, OWN, pl.ds(0, NS - 1)], a1_ss.at[it], a1_rs.at[it, 0]).wait_send()
        waiter(zg.at[it, pl.ds(0, 13)], a2_ss.at[it], a2_rs.at[it, 0]).wait_send()

    gains_out(0)
    for k in range(NS - 1):
        remote(csend.at[mates[k]], crecv.at[s], c_ss, c_rs.at[s], device(mates[k])).start()
    crecv[s] = csend[s]
    for load in loads[6:]:
        load.wait()
    to_pieces(m_ref, state_m)
    to_pieces(v_ref, state_v)
    gains_on(0)

    sources = [s] + mates[::-1]
    row_id = lax.broadcasted_iota(I32, (ROWS, NBL), 0)

    for i, source in enumerate(sources):
        if i:
            waiter(crecv.at[source], c_ss, c_rs.at[source]).wait_recv()
        for k in range(2):
            row = crecv[source, 134 + k : 135 + k, :].astype(I32)
            pick[:, 256 * i + 128 * k : 256 * i + 128 * k + 128] = jnp.where(row_id == row, 1.0, 0.0).astype(BF16)

    lane32 = lax.broadcasted_iota(I32, (32, 128), 1)
    odd32 = (lane32 & 32) != 0
    odd8 = (lane8 & 32) != 0
    pair32 = lax.broadcasted_iota(I32, (32, 128), 0) >> 2
    chan = 2 * pair32 + jnp.where(odd32, 1, 0)
    a1 = math.exp(-DECAY)

    def decay(steps):
        return jnp.exp(-DECAY * steps.astype(F32))

    whole_chan = chan + 16 * x
    geometric = 1.0 / (1.0 - a1)
    norm = (1.0 - decay(whole_chan + 1)) * geometric + (a1 - decay(NCHAN - whole_chan)) * geometric
    half_norm = BLEND / norm
    from_left = decay(chan + 1)
    from_right = decay(16 - chan)
    near_left = jnp.where(odd32, a1 * a1, a1)
    near_right = jnp.where(odd32, a1, a1 * a1)
    up = jnp.where(odd32, 1.0, a1)
    down = jnp.where(odd32, a1, 1.0)

    def swap(value):
        return jnp.where((lax.broadcasted_iota(I32, value.shape, 1) & 32) != 0, pltpu.roll(value, 32, 1), pltpu.roll(value, 96, 1))

    def smooth(it):
        total = tots[...]
        swapped = swap(total)
        right_going = total * up + swapped * down
        left_going = total * down + swapped * up
        blended = total + a1 * swapped
        zero = jnp.zeros((4, 128), F32)
        lefts, rights = [zero], [zero]
        for k in range(NS):
            lefts.append(a1 * a1 * lefts[-1] + right_going[4 * k : 4 * k + 4])
            q = NS - 1 - k
            rights.append(a1 * a1 * rights[-1] + left_going[4 * q : 4 * q + 4])
        out8 = jnp.concatenate([jnp.where(odd8[0:4], rights[NS], lefts[NS])] * 2, axis=0)
        xs[it] = out8[0:4]
        for dx in (2, 1, 3):
            remote(xs.at[it], xr.at[it, dx - 1], x_ss.at[it], x_rs.at[it], device(s, 0, dx)).start()
        left_all = jnp.concatenate(lefts[:NS], axis=0)
        right_all = jnp.concatenate(rights[NS - 1 :: -1], axis=0)
        blended = blended + near_left * left_all + near_right * right_all
        across = jnp.zeros((4, 128), F32)
        weights = []
        for dx in (1, 2, 3):
            source = lax.rem(x - dx + NX, NX)
            gap = jnp.full((8, 128), jnp.abs(x - source), I32)
            is_left = jnp.full((8, 128), x - source, I32) > 0
            used = jnp.where(is_left, jnp.where(odd8, 0, 1), jnp.where(odd8, 1, 0)).astype(F32)
            weights.append((used * decay(16 * (gap - 1)))[0:4])
        waiter(xr.at[it], x_ss.at[it], x_rs.at[it]).wait_recv()
        for dx in (1, 2, 3):
            across = across + xr[it, dx - 1] * weights[dx - 1]
        across = jnp.concatenate([across] * 8, axis=0)
        other = swap(across)
        blended = blended + from_left * jnp.where(odd32, other, across) + from_right * jnp.where(odd32, across, other)
        return (1.0 - BLEND) * total + half_norm * blended

    coef = -2.0 / math.sqrt(2.0 * NBL * NS * NZ / (4 * NS * NZ))

    for it in range(ITERS):
        last = it == ITERS - 1
        gains_in(it)
        for t in range(4):
            block = zg[it, 4 * t : 4 * t + 4].reshape(128, 128).T
            high = block.astype(BF16)
            gsplit[0:128, 128 * t : 128 * t + 128] = high
            gsplit[128:256, 128 * t : 128 * t + 128] = (block - high.astype(F32)).astype(BF16)

        for i, source in enumerate(sources):
            both = jnp.dot(gsplit[...], pick[:, 256 * i : 256 * i + 256], preferred_element_type=F32)
            both = both[0:128] + both[128:256]
            ga, gb = both[0:64, 0:128], both[64:128, 0:128]
            gc, gd = both[0:64, 128:256], both[64:128, 128:256]
            cr, ci = crecv[source, 0:64, :], crecv[source, 64:128, :]
            u = ga * gc + gb * gd
            v = gb * gc - ga * gd
            model_re = jnp.sum((u * cr - v * ci).reshape(2, SKY_SOURCES, NBL), axis=1)
            model_im = jnp.sum((u * ci + v * cr).reshape(2, SKY_SOURCES, NBL), axis=1)
            weight = crecv[source, 132:134, :]
            err_re = weight * (crecv[source, 128:130, :] - model_re)
            err_im = weight * (crecv[source, 130:132, :] - model_im)
            if last:
                ressend[source] = jnp.concatenate([err_re, err_im], axis=0)
            wide = (2, SKY_SOURCES, NBL)
            sr = jnp.broadcast_to((coef * err_re)[:, None, :], wide).reshape(64, NBL)
            si = jnp.broadcast_to((coef * err_im)[:, None, :], wide).reshape(64, NBL)
            px = gc * cr + gd * ci
            py = gd * cr - gc * ci
            qx = ga * cr - gb * ci
            qy = ga * ci + gb * cr
            terms = ((sr * px - si * py, sr * py + si * px), (sr * qx + si * qy, sr * qy - si * qx))
            for k in range(2):
                for ri in range(2):
                    value = terms[k][ri]
                    high = value.astype(BF16)
                    where = pl.ds(256 * i + 128 * k, 128)
                    grads[64 * ri : 64 * ri + 64, where] = high
                    grads[128 + 64 * ri : 192 + 64 * ri, where] = (value - high.astype(F32)).astype(BF16)

        def station_sums(begin, end):
            both = lax.dot_general(
                pick[begin:end, :], grads[...], (((1,), (1,)), ((), ())), preferred_element_type=F32
            )
            zp[it, begin:end, :] = both[:, 0:128] + both[:, 128:256]

        station_sums(0, 32 * OWN)
        for i, n in enumerate(STEPS):
            remote(zp.at[it, pl.ds(64 + 64 * i, 64)], rsn.at[it, i], r1_ss.at[it], r1_rs.at[it], device(s, -n)).start()
        for h in range(2):
            remote(zp.at[it, pl.ds(320 + 16 * h, 16)], rsh.at[it, h], rh_ss.at[it], rh_rs.at[it], device(s, 6 * h - 3)).start()
        station_sums(32 * OWN, ROWS)
        for i, n in enumerate(STEPS):
            remote(zp.at[it, pl.ds(384 + 32 * i, 32)], rsc.at[it, i], rc_ss.at[it], rc_rs.at[it], device(s, -n)).start()
        if last:
            for k in range(NS - 1):
                remote(ressend.at[mates[k]], resrecv.at[s], o_ss, o_rs, device(mates[k])).start()
            resrecv[s] = ressend[s]
        else:
            waiter(csend.at[pl.ds(0, NS - 1)], c_ss, c_rs.at[s]).wait_send()
        gains_sent(it)
        near = waiter(rsn.at[it], r1_ss.at[it], r1_rs.at[it])
        half = waiter(rsh.at[it], rh_ss.at[it], rh_rs.at[it])
        own = waiter(rsc.at[it], rc_ss.at[it], rc_rs.at[it])
        def far_out(j, acc):
            for k in range(NS):
                accp[it, j, k] = acc[4 * k : 4 * k + 4]
            for k in [*range(NS - 1)] + ([None] if j != 2 else []):
                to = s if k is None else mates[k]
                remote(
                    accp.at[it, j, to], rsp.at[it, j, s], r2_ss.at[it], r2_rs.at[it, j], device(to, CENTRES[j])
                ).start()

        near.wait_recv()
        half.wait_recv()
        acc = zp[it, 0:64, :]
        for i in range(len(STEPS)):
            acc = acc + rsn[it, i]
        far_out(0, jnp.concatenate([acc[0:16] + rsh[it, 0], acc[16:32]], axis=0))
        far_out(1, jnp.concatenate([acc[32:48], acc[48:64] + rsh[it, 1]], axis=0))
        own.wait_recv()
        acc = zp[it, 32 * OWN : 32 * OWN + 32, :]
        for i in range(len(STEPS)):
            acc = acc + rsc[it, i]
        far_out(2, acc)
        rsp[it, 2, s] = accp[it, 2, s]
        near.wait_send()
        half.wait_send()
        own.wait_send()
        if last:
            result = waiter(resrecv.at[pl.ds(0, NS - 1)], o_ss, o_rs)
            result.wait_send()
            result.wait_recv()
            for k in range(NS):
                for ri in range(2):
                    res_ref[ri, 2 * k : 2 * k + 2, :] = resrecv[k, 2 * ri : 2 * ri + 2, :]
        waiter(rsp.at[it, 2, pl.ds(0, NS - 1)], r2_ss.at[it], r2_rs.at[it, 2]).wait_recv()
        for j in range(2):
            waiter(rsp.at[it, j], r2_ss.at[it], r2_rs.at[it, j]).wait_recv()
        for k in range(NS):
            tots[4 * k : 4 * k + 4, :] = rsp[it, 0, k] + rsp[it, 1, k] + rsp[it, 2, k]

        smoothed = smooth(it)
        tally = STEP + it + 1
        new_m = BETA_ONE * state_m[...] + (1.0 - BETA_ONE) * smoothed
        new_v = BETA_TWO * state_v[...] + (1.0 - BETA_TWO) * smoothed * smoothed
        first_hat = new_m / (1.0 - BETA_ONE**tally)
        second_hat = new_v / (1.0 - BETA_TWO**tally)
        new_g = state_g[...] - LEARN_RATE * first_hat / (jnp.sqrt(second_hat) + ADAM_EPSILON)
        if last:
            from_pieces(new_g, go_ref)
            from_pieces(new_m, mo_ref)
            from_pieces(new_v, vo_ref)
        else:
            for k in range(NS):
                gpiece[it + 1, k] = new_g[4 * k : 4 * k + 4]
            gains_out(it + 1)
            state_g[...] = new_g
            state_m[...] = new_m
            state_v[...] = new_v
        waiter(rsp.at[it, pl.ds(0, 2)], r2_ss.at[it], r2_rs.at[it, 0]).wait_send()
        waiter(rsp.at[it, 2, pl.ds(0, NS - 1)], r2_ss.at[it], r2_rs.at[it, 2]).wait_send()
        waiter(xr.at[it], x_ss.at[it], x_rs.at[it]).wait_send()
        if not last:
            gains_on(it + 1)


def store(*refs):
    sem = refs[-1]
    copies = [pltpu.make_async_copy(refs[i], refs[4 + i], sem.at[i]) for i in range(4)]
    for copy in copies:
        copy.start()
    for copy in copies:
        copy.wait()


def on_device(coherency, measured, rejected, pairs, fetch_lists, gains, first, second):
    args = (
        coherency, jnp.swapaxes(measured, 1, 2), rejected.T, pairs.T, fetch_lists.T, gains, first, second,
    )
    args = [pltpu.with_memory_space_constraint(a, pltpu.HBM) for a in args]
    out = [jax.ShapeDtypeStruct(gains.shape, F32)] * 3 + [jax.ShapeDtypeStruct(args[1].shape, F32)]
    vmem = pl.BlockSpec(memory_space=pltpu.VMEM)
    anywhere = pl.BlockSpec(memory_space=pl.ANY)
    hbm = pl.BlockSpec(memory_space=pltpu.HBM)
    sem = pltpu.SemaphoreType.DMA
    buf = pltpu.VMEM
    results = pl.pallas_call(
        kernel,
        out_shape=out,
        in_specs=[hbm] * 8,
        out_specs=[vmem] * 4,
        scratch_shapes=[
            *[buf(a.shape, a.dtype) for a in args],
            sem((8,)),
            buf((NS, CROWS, NBL), F32),
            buf((NS, CROWS, NBL), F32),
            buf((ROWS, 2 * NBL * NS), BF16),
            buf((256, ROWS), BF16),
            buf((256, 2 * NBL * NS), BF16),
            buf((32, 128), F32),
            buf((32, 128), F32),
            buf((32, 128), F32),
            buf((ITERS, NS, 4, 128), F32),
            buf((ITERS, NZ, NS, 4, 128), F32),
            buf((ITERS, ROWS, 128), F32),
            buf((ITERS, 4, 64, 128), F32),
            buf((ITERS, 4, 32, 128), F32),
            buf((ITERS, 2, 16, 128), F32),
            buf((ITERS, 3, NS, 4, 128), F32),
            buf((ITERS, 3, NS, 4, 128), F32),
            buf((32, 128), F32),
            buf((ITERS, 4, 128), F32),
            buf((ITERS, 3, 4, 128), F32),
            buf((NS, 4, 128), F32),
            buf((NS, 4, 128), F32),
            sem, sem((NS,)),
            sem((ITERS,)), sem((ITERS, 3)),
            sem((ITERS,)), sem((ITERS, 2)),
            sem((ITERS,)), sem((ITERS,)),
            sem((ITERS,)), sem((ITERS,)),
            sem((ITERS,)), sem((ITERS,)),
            sem((ITERS,)), sem((ITERS, 3)),
            sem((ITERS,)), sem((ITERS,)),
            sem, sem,
        ],
        compiler_params=pltpu.CompilerParams(collective_id=0, has_side_effects=True, vmem_limit_bytes=32 * 2**20),
        cost_estimate=pl.CostEstimate(flops=4 * 10**9, bytes_accessed=2**20, transcendentals=10**4),
        name="calibrate",
    )(*args)
    new_g, new_m, new_v, residual = pl.pallas_call(
        store, out_shape=out, in_specs=[anywhere] * 4, out_specs=[hbm] * 4, scratch_shapes=[sem((4,))], name="store",
        compiler_params=pltpu.CompilerParams(vmem_limit_bytes=32 * 2**20),
    )(*results)
    return new_g, new_m, new_v, jnp.swapaxes(residual, 1, 2)


def solution(mesh):
    split = P(None, "bl", "ch")
    return jax.shard_map(
        on_device,
        mesh=mesh,
        in_specs=(split, split, P("bl", "ch"), P("bl", None), P(), split, split, split),
        out_specs=(split,) * 4,
        check_vma=False,
    )
```

time: 90.7 us -> 79.2 us (0.87)
  Pallas kernels: 84.6 us -> 78.4 us
  local copies, waits for them, and re-layouts: 5.15 us -> 0 us
    pallas_call x1 -> x2, Pallas kernels: 84.6 us -> 78.4 us  [the longest x1 77.7 us: on_device(): pl.pallas_call(kernel, out_shape=out, in_specs=[hbm] * 8, out_specs=[vmem...]
    unnamed x17 -> x0, local copies, waits for them, and re-layouts: 4.47 us -> none
where the time goes in v2:
time: 79.2 us; the launch traced here: 79 us
  Pallas kernels  78.4 us (99%)
    pallas_call x1, Pallas kernels, on_device(): pl.pallas_call(kernel, out_shape=out, in_specs=[hbm] * 8, out_specs=[vmem...  77.7 us

profile of v2, /device:TPU:1, one launch (start us, length us, event | category | flops | bytes accessed | tf_op | source)
XLA Modules:
  0.0 79.0 jit_solution(11892732083567275010)
XLA Ops:
  0.6 77.7 %calibrate.1 = (f32[2,4,512]{2,1,0:T(4,128)S(1)}, f32[2,4,512]{2,1,0:T(4,128)S(1)}, f32[2,4,512]{2,1,0:T(4,128)S(1)}, f32[2,16,128]{2,1,0:T(8,128)S(1)}) custom-call(bf16[2,128,512]{2,1,0:T(8,128)(2,1)} %c_hbm.1, f32[2,16,128]{2,1,0:T(8,128)} %bitcast.6, s32[16,128]{1,0:T(8,128)} %bitcast.8, s32[2,128]{1,0:T(2,128)} %bitcast.9, s32[64,128]{1,0:T(8,128)} %bitcast.5, ...), custom_call_target="tpu_custom_call" | custom-call | flops 4000000000 | bytes 1048576 | tf_op jit(solution)/shard_map/calibrate/pallas_call | solution.py:415
  78.4 0.7 store.1

commit v3 on v2

--- a/solution.py
+++ b/solution.py
@@ -22,14 +22,15 @@
 
 NX, NY, NZ, NS = 4, 4, 16, 8
 NCHAN = 64
-FAR = 5
-CENTRES = (-FAR, FAR, 0)
-STEPS = (1, -1, 2, -2)
-ORDER = [-FAR, FAR] + [j - n for n in STEPS for j in (-FAR, FAR)] + [8] + [0] + [-n for n in STEPS]
+CENTRES = (-6, 6, -3, 3, 0)
+STEPS = (1, -1)
+ORDER = [-6, 6] + [j - n for n in STEPS for j in (-6, 6)] + [8] + [-3, 3, 0] + [j - n for n in STEPS for j in (-3, 3, 0)]
 SLOT = {rel % NZ: slot for slot, rel in enumerate(ORDER)}
-OPPOSITE, OWN = 10, 11
-HOME = (0, 1, OWN)
-BACK = (1, 0, OWN)
+OPPOSITE, OWN = 6, 9
+FIRST = 7
+BACK = (1, 0, 8, 7, OWN)
+GROUP = (1, 0, 2, 2, 3)
+NC = len(CENTRES)
 ROWS = 32 * NZ
 PLANE = ((2, 0), (2, 1), (1, 0), (3, 0), (1, 1), (3, 1), (0, 1))
 NBL = 128
@@ -52,21 +53,19 @@
     c_ss, c_rs, a1_ss, a1_rs, a2_ss, a2_rs, r1_ss, r1_rs, rc_ss, rc_rs, rh_ss, rh_rs, r2_ss, r2_rs, x_ss, x_rs, o_ss, o_rs,
 ):
     bl, x = lax.axis_index("bl"), lax.axis_index("ch")
-    y, z, c = lax.div(bl, 2 * NZ), lax.rem(lax.div(bl, 2), NZ), lax.rem(bl, 2)
+    y, z, c = bl >> 5, (bl >> 1) & (NZ - 1), bl & 1
     s = 2 * y + c
-
-    def device(s_to, dz=0, dx=0):
-        z_to, x_to = lax.rem(z + dz + NZ, NZ), lax.rem(x + dx, NX)
-        return ((lax.div(s_to, 2) * NZ + z_to) * 2 + lax.rem(s_to, 2), x_to)
-
-    def mate(dy, dc):
-        return 2 * lax.rem(y + dy, NY) + lax.rem(c + dc, 2)
-
-    mates = [mate(dy, dc) for dy, dc in PLANE]
+    mates = [2 * ((y + dy) & (NY - 1)) + (c ^ dc) for dy, dc in PLANE]
+    plane_at = {dz: 2 * ((z + dz) & (NZ - 1)) for dz in (0, 1, -1, 2, -2, 3, -3, 6, -6)}
+    column_of = [32 * ((y + dy) & (NY - 1)) + (c ^ dc) for dy, dc in PLANE] + [32 * y + c]
+
+    def device(k, dz=0, dx=0):
+        k = NS - 1 if k is None else k
+        return (column_of[k] + plane_at[dz], (x + dx) & (NX - 1) if dx else x)
 
     barrier = pltpu.get_barrier_semaphore()
-    partners = [device(s, j) if k == NS - 1 else device(mates[k], j) for j in CENTRES for k in range(NS) if j or k < NS - 1]
-    partners += [device(s, n) for n in (1, -1, 2, -2, 3, -3)] + [device(s, 0, dx) for dx in (1, 2, 3)]
+    partners = [device(k, j) for j in CENTRES for k in range(NS) if j or k < NS - 1]
+    partners += [device(None, n) for n in (2, -2, 1, -1)] + [device(None, 0, dx) for dx in (1, 2, 3)]
     for partner in partners:
         pl.semaphore_signal(barrier, inc=1, device_id=partner, device_id_type=MESH)
 
@@ -141,52 +140,50 @@
     pl.semaphore_wait(barrier, len(partners))
 
     def waiter(ref, send_sem, recv_sem):
-        return remote(ref, ref, send_sem, recv_sem, device(mates[0]))
+        return remote(ref, ref, send_sem, recv_sem, device(0))
 
     def gains_out(it):
-        for j in range(3):
-            for k in [*range(NS - 1)] + ([None] if j != 2 else []):
+        for j in range(NC):
+            for k in [*range(NS - 1)] + ([None] if CENTRES[j] else []):
                 to = s if k is None else mates[k]
                 remote(
-                    gpiece.at[it, to], zg.at[it, BACK[j], s], a1_ss.at[it], a1_rs.at[it, (1, 0, 2)[j]], device(to, CENTRES[j])
+                    gpiece.at[it, to], zg.at[it, BACK[j], s], a1_ss.at[it], a1_rs.at[it, GROUP[j]], device(k, CENTRES[j])
                 ).start()
 
     def gains_on(it):
-        def near_copy(i, own):
-            width = 1 if own else 2
-            src, dst = (OWN, OWN + 1 + i) if own else (0, 2 + 2 * i)
-            return remote(
-                zg.at[it, pl.ds(src, width)], zg.at[it, pl.ds(dst, width)], a2_ss.at[it], a2_rs.at[it, own], device(s, STEPS[i])
-            )
-
-        def half_copy(h):
-            half = pl.ds(4 * h, 4)
-            return remote(
-                zg.at[it, h, half], zg.at[it, OPPOSITE, half], a2_ss.at[it], a2_rs.at[it, 0], device(s, 3 - 6 * h)
-            )
+        def near_copy(src, width, dst, part, n):
+            remote(
+                zg.at[it, pl.ds(src, width)], zg.at[it, pl.ds(dst, width)], a2_ss.at[it], a2_rs.at[it, part], device(None, n)
+            ).start()
 
         zg[it, OWN, s] = gpiece[it, s]
-        waiter(zg.at[it, OWN, pl.ds(0, NS - 1)], a1_ss.at[it], a1_rs.at[it, 2]).wait_recv()
-        for i in range(len(STEPS)):
-            near_copy(i, 1).start()
+        waiter(zg.at[it, OWN, pl.ds(0, NS - 1)], a1_ss.at[it], a1_rs.at[it, 3]).wait_recv()
+        for i, n in enumerate(STEPS):
+            near_copy(OWN, 1, 12 + 3 * i, 1, n)
+        waiter(zg.at[it, pl.ds(7, 2)], a1_ss.at[it], a1_rs.at[it, 2]).wait_recv()
+        for i, n in enumerate(STEPS):
+            near_copy(7, 2, 10 + 3 * i, 1, n)
         for h in range(2):
             waiter(zg.at[it, h], a1_ss.at[it], a1_rs.at[it, h]).wait_recv()
-            half_copy(h).start()
-        for i in range(len(STEPS)):
-            near_copy(i, 0).start()
+            half = pl.ds(4 * h, 4)
+            remote(
+                zg.at[it, h, half], zg.at[it, OPPOSITE, half], a2_ss.at[it], a2_rs.at[it, 0], device(None, 2 - 4 * h)
+            ).start()
+        for i, n in enumerate(STEPS):
+            near_copy(0, 2, 2 + 2 * i, 0, n)
 
     def gains_in(it):
-        waiter(zg.at[it, pl.ds(OWN + 1, 4)], a2_ss.at[it], a2_rs.at[it, 1]).wait_recv()
-        waiter(zg.at[it, pl.ds(2, 9)], a2_ss.at[it], a2_rs.at[it, 0]).wait_recv()
+        waiter(zg.at[it, pl.ds(10, 6)], a2_ss.at[it], a2_rs.at[it, 1]).wait_recv()
+        waiter(zg.at[it, pl.ds(2, 5)], a2_ss.at[it], a2_rs.at[it, 0]).wait_recv()
 
     def gains_sent(it):
-        waiter(zg.at[it, pl.ds(0, 2)], a1_ss.at[it], a1_rs.at[it, 0]).wait_send()
+        waiter(zg.at[it, pl.ds(0, 4)], a1_ss.at[it], a1_rs.at[it, 0]).wait_send()
         waiter(zg.at[it, OWN, pl.ds(0, NS - 1)], a1_ss.at[it], a1_rs.at[it, 0]).wait_send()
-        waiter(zg.at[it, pl.ds(0, 13)], a2_ss.at[it], a2_rs.at[it, 0]).wait_send()
+        waiter(zg.at[it, pl.ds(0, 11)], a2_ss.at[it], a2_rs.at[it, 0]).wait_send()
 
     gains_out(0)
     for k in range(NS - 1):
-        remote(csend.at[mates[k]], crecv.at[s], c_ss, c_rs.at[s], device(mates[k])).start()
+        remote(csend.at[mates[k]], crecv.at[s], c_ss, c_rs.at[s], device(k)).start()
     crecv[s] = csend[s]
     for load in loads[6:]:
         load.wait()
@@ -224,6 +221,17 @@
     near_right = jnp.where(odd32, a1, a1 * a1)
     up = jnp.where(odd32, 1.0, a1)
     down = jnp.where(odd32, a1, 1.0)
+    to_edge = decay(2 * jnp.where(odd32, pair32, NS - 1 - pair32))
+    edge_same = jnp.where(odd32, down, up) * to_edge
+    edge_other = jnp.where(odd32, up, down) * to_edge
+    take_left, take_right = half_norm * from_left, half_norm * from_right
+    weights = []
+    for dx in (1, 2, 3):
+        source = (x - dx) & (NX - 1)
+        gap = jnp.full((8, 128), jnp.abs(x - source), I32)
+        is_left = jnp.full((8, 128), x - source, I32) > 0
+        used = jnp.where(is_left, jnp.where(odd8, 0, 1), jnp.where(odd8, 1, 0)).astype(F32)
+        weights.append((used * decay(16 * (gap - 1)))[0:4])
 
     def swap(value):
         return jnp.where((lax.broadcasted_iota(I32, value.shape, 1) & 32) != 0, pltpu.roll(value, 32, 1), pltpu.roll(value, 96, 1))
@@ -231,37 +239,30 @@
     def smooth(it):
         total = tots[...]
         swapped = swap(total)
+        edge = total * edge_same + swapped * edge_other
+        edge = (edge[0:8] + edge[8:16]) + (edge[16:24] + edge[24:32])
+        xs[it] = edge[0:4] + edge[4:8]
+        for dx in (2, 1, 3):
+            remote(xs.at[it], xr.at[it, dx - 1], x_ss.at[it], x_rs.at[it], device(None, 0, dx)).start()
         right_going = total * up + swapped * down
         left_going = total * down + swapped * up
-        blended = total + a1 * swapped
         zero = jnp.zeros((4, 128), F32)
         lefts, rights = [zero], [zero]
-        for k in range(NS):
+        for k in range(NS - 1):
             lefts.append(a1 * a1 * lefts[-1] + right_going[4 * k : 4 * k + 4])
             q = NS - 1 - k
             rights.append(a1 * a1 * rights[-1] + left_going[4 * q : 4 * q + 4])
-        out8 = jnp.concatenate([jnp.where(odd8[0:4], rights[NS], lefts[NS])] * 2, axis=0)
-        xs[it] = out8[0:4]
-        for dx in (2, 1, 3):
-            remote(xs.at[it], xr.at[it, dx - 1], x_ss.at[it], x_rs.at[it], device(s, 0, dx)).start()
-        left_all = jnp.concatenate(lefts[:NS], axis=0)
-        right_all = jnp.concatenate(rights[NS - 1 :: -1], axis=0)
-        blended = blended + near_left * left_all + near_right * right_all
-        across = jnp.zeros((4, 128), F32)
-        weights = []
-        for dx in (1, 2, 3):
-            source = lax.rem(x - dx + NX, NX)
-            gap = jnp.full((8, 128), jnp.abs(x - source), I32)
-            is_left = jnp.full((8, 128), x - source, I32) > 0
-            used = jnp.where(is_left, jnp.where(odd8, 0, 1), jnp.where(odd8, 1, 0)).astype(F32)
-            weights.append((used * decay(16 * (gap - 1)))[0:4])
+        left_all = jnp.concatenate(lefts, axis=0)
+        right_all = jnp.concatenate(rights[::-1], axis=0)
+        blended = total + a1 * swapped + near_left * left_all + near_right * right_all
+        smoothed = (1.0 - BLEND) * total + half_norm * blended
         waiter(xr.at[it], x_ss.at[it], x_rs.at[it]).wait_recv()
-        for dx in (1, 2, 3):
-            across = across + xr[it, dx - 1] * weights[dx - 1]
-        across = jnp.concatenate([across] * 8, axis=0)
+        across = xr[it, 0] * weights[0] + xr[it, 1] * weights[1] + xr[it, 2] * weights[2]
+        across = jnp.concatenate([across] * 2, axis=0)
         other = swap(across)
-        blended = blended + from_left * jnp.where(odd32, other, across) + from_right * jnp.where(odd32, across, other)
-        return (1.0 - BLEND) * total + half_norm * blended
+        left = jnp.concatenate([jnp.where(odd8, other, across)] * 4, axis=0)
+        right = jnp.concatenate([jnp.where(odd8, across, other)] * 4, axis=0)
+        return smoothed + take_left * left + take_right * right
 
     coef = -2.0 / math.sqrt(2.0 * NBL * NS * NZ / (4 * NS * NZ))
 
@@ -311,17 +312,19 @@
             )
             zp[it, begin:end, :] = both[:, 0:128] + both[:, 128:256]
 
-        station_sums(0, 32 * OWN)
+        station_sums(0, 32 * FIRST)
         for i, n in enumerate(STEPS):
-            remote(zp.at[it, pl.ds(64 + 64 * i, 64)], rsn.at[it, i], r1_ss.at[it], r1_rs.at[it], device(s, -n)).start()
+            remote(zp.at[it, pl.ds(64 + 64 * i, 64)], rsn.at[it, i], r1_ss.at[it], r1_rs.at[it], device(None, -n)).start()
         for h in range(2):
-            remote(zp.at[it, pl.ds(320 + 16 * h, 16)], rsh.at[it, h], rh_ss.at[it], rh_rs.at[it], device(s, 6 * h - 3)).start()
-        station_sums(32 * OWN, ROWS)
+            remote(
+                zp.at[it, pl.ds(32 * OPPOSITE + 16 * h, 16)], rsh.at[it, h], rh_ss.at[it], rh_rs.at[it], device(None, 4 * h - 2)
+            ).start()
+        station_sums(32 * FIRST, ROWS)
         for i, n in enumerate(STEPS):
-            remote(zp.at[it, pl.ds(384 + 32 * i, 32)], rsc.at[it, i], rc_ss.at[it], rc_rs.at[it], device(s, -n)).start()
+            remote(zp.at[it, pl.ds(320 + 96 * i, 96)], rsc.at[it, i], rc_ss.at[it], rc_rs.at[it], device(None, -n)).start()
         if last:
             for k in range(NS - 1):
-                remote(ressend.at[mates[k]], resrecv.at[s], o_ss, o_rs, device(mates[k])).start()
+                remote(ressend.at[mates[k]], resrecv.at[s], o_ss, o_rs, device(k)).start()
             resrecv[s] = ressend[s]
         else:
             waiter(csend.at[pl.ds(0, NS - 1)], c_ss, c_rs.at[s]).wait_send()
@@ -332,25 +335,22 @@
         def far_out(j, acc):
             for k in range(NS):
                 accp[it, j, k] = acc[4 * k : 4 * k + 4]
-            for k in [*range(NS - 1)] + ([None] if j != 2 else []):
+            for k in [*range(NS - 1)] + ([None] if CENTRES[j] else []):
                 to = s if k is None else mates[k]
                 remote(
-                    accp.at[it, j, to], rsp.at[it, j, s], r2_ss.at[it], r2_rs.at[it, j], device(to, CENTRES[j])
+                    accp.at[it, j, to], rsp.at[it, j, s], r2_ss.at[it], r2_rs.at[it, (0, 3, 1, 1, 2)[j]], device(k, CENTRES[j])
                 ).start()
 
         near.wait_recv()
         half.wait_recv()
-        acc = zp[it, 0:64, :]
-        for i in range(len(STEPS)):
-            acc = acc + rsn[it, i]
+        acc = zp[it, 0:64, :] + rsn[it, 0] + rsn[it, 1]
         far_out(0, jnp.concatenate([acc[0:16] + rsh[it, 0], acc[16:32]], axis=0))
         far_out(1, jnp.concatenate([acc[32:48], acc[48:64] + rsh[it, 1]], axis=0))
         own.wait_recv()
-        acc = zp[it, 32 * OWN : 32 * OWN + 32, :]
-        for i in range(len(STEPS)):
-            acc = acc + rsc[it, i]
-        far_out(2, acc)
-        rsp[it, 2, s] = accp[it, 2, s]
+        acc = zp[it, 32 * FIRST : 32 * FIRST + 96, :] + rsc[it, 0] + rsc[it, 1]
+        for j in (2, 3, 4):
+            far_out(j, acc[32 * j - 64 : 32 * j - 32])
+        rsp[it, NC - 1, s] = accp[it, NC - 1, s]
         near.wait_send()
         half.wait_send()
         own.wait_send()
@@ -361,11 +361,14 @@
             for k in range(NS):
                 for ri in range(2):
                     res_ref[ri, 2 * k : 2 * k + 2, :] = resrecv[k, 2 * ri : 2 * ri + 2, :]
-        waiter(rsp.at[it, 2, pl.ds(0, NS - 1)], r2_ss.at[it], r2_rs.at[it, 2]).wait_recv()
-        for j in range(2):
-            waiter(rsp.at[it, j], r2_ss.at[it], r2_rs.at[it, j]).wait_recv()
+        waiter(rsp.at[it, NC - 1, pl.ds(0, NS - 1)], r2_ss.at[it], r2_rs.at[it, 2]).wait_recv()
+        waiter(rsp.at[it, pl.ds(2, 2)], r2_ss.at[it], r2_rs.at[it, 1]).wait_recv()
         for k in range(NS):
-            tots[4 * k : 4 * k + 4, :] = rsp[it, 0, k] + rsp[it, 1, k] + rsp[it, 2, k]
+            tots[4 * k : 4 * k + 4, :] = rsp[it, 4, k] + rsp[it, 2, k] + rsp[it, 3, k]
+        for j in (0, 1):
+            waiter(rsp.at[it, j], r2_ss.at[it], r2_rs.at[it, j and 3]).wait_recv()
+        for k in range(NS):
+            tots[4 * k : 4 * k + 4, :] += rsp[it, 0, k] + rsp[it, 1, k]
 
         smoothed = smooth(it)
         tally = STEP + it + 1
@@ -385,8 +388,8 @@
             state_g[...] = new_g
             state_m[...] = new_m
             state_v[...] = new_v
-        waiter(rsp.at[it, pl.ds(0, 2)], r2_ss.at[it], r2_rs.at[it, 0]).wait_send()
-        waiter(rsp.at[it, 2, pl.ds(0, NS - 1)], r2_ss.at[it], r2_rs.at[it, 2]).wait_send()
+        waiter(rsp.at[it, pl.ds(0, NC - 1)], r2_ss.at[it], r2_rs.at[it, 0]).wait_send()
+        waiter(rsp.at[it, NC - 1, pl.ds(0, NS - 1)], r2_ss.at[it], r2_rs.at[it, 2]).wait_send()
         waiter(xr.at[it], x_ss.at[it], x_rs.at[it]).wait_send()
         if not last:
             gains_on(it + 1)
@@ -431,23 +434,23 @@
             buf((ITERS, NS, 4, 128), F32),
             buf((ITERS, NZ, NS, 4, 128), F32),
             buf((ITERS, ROWS, 128), F32),
-            buf((ITERS, 4, 64, 128), F32),
-            buf((ITERS, 4, 32, 128), F32),
+            buf((ITERS, 2, 64, 128), F32),
+            buf((ITERS, 2, 96, 128), F32),
             buf((ITERS, 2, 16, 128), F32),
-            buf((ITERS, 3, NS, 4, 128), F32),
-            buf((ITERS, 3, NS, 4, 128), F32),
+            buf((ITERS, NC, NS, 4, 128), F32),
+            buf((ITERS, NC, NS, 4, 128), F32),
             buf((32, 128), F32),
             buf((ITERS, 4, 128), F32),
             buf((ITERS, 3, 4, 128), F32),
             buf((NS, 4, 128), F32),
             buf((NS, 4, 128), F32),
             sem, sem((NS,)),
-            sem((ITERS,)), sem((ITERS, 3)),
+            sem((ITERS,)), sem((ITERS, 4)),
             sem((ITERS,)), sem((ITERS, 2)),
             sem((ITERS,)), sem((ITERS,)),
             sem((ITERS,)), sem((ITERS,)),
             sem((ITERS,)), sem((ITERS,)),
-            sem((ITERS,)), sem((ITERS, 3)),
+            sem((ITERS,)), sem((ITERS, 4)),
             sem((ITERS,)), sem((ITERS,)),
             sem, sem,
         ],

time: 79.2 us -> 75.4 us (0.952)
  Pallas kernels: 78.4 us -> 74.6 us
    pallas_call x1, Pallas kernels: 77.7 us -> 73.9 us  [on_device(): pl.pallas_call(kernel, out_shape=out, in_specs=[hbm] * 8, out_specs=[vmem...]
where the time goes in v3:
time: 75.4 us; the launch traced here: 75.2 us
  Pallas kernels  74.6 us (99%)
    pallas_call x1, Pallas kernels, on_device(): pl.pallas_call(kernel, out_shape=out, in_specs=[hbm] * 8, out_specs=[vmem...  73.9 us

profile of v3, /device:TPU:1, one launch (start us, length us, event | category | flops | bytes accessed | tf_op | source)
XLA Modules:
  0.0 75.2 jit_solution(10875786440032341057)
XLA Ops:
  0.6 73.9 %calibrate.1 = (f32[2,4,512]{2,1,0:T(4,128)S(1)}, f32[2,4,512]{2,1,0:T(4,128)S(1)}, f32[2,4,512]{2,1,0:T(4,128)S(1)}, f32[2,16,128]{2,1,0:T(8,128)S(1)}) custom-call(bf16[2,128,512]{2,1,0:T(8,128)(2,1)} %c_hbm.1, f32[2,16,128]{2,1,0:T(8,128)} %bitcast.6, s32[16,128]{1,0:T(8,128)} %bitcast.8, s32[2,128]{1,0:T(2,128)} %bitcast.9, s32[64,128]{1,0:T(8,128)} %bitcast.5, ...), custom_call_target="tpu_custom_call" | custom-call | flops 4000000000 | bytes 1048576 | tf_op jit(solution)/shard_map/calibrate/pallas_call | solution.py:418
  74.6 0.7 store.1

commit v4 on v3

--- a/solution.py
+++ b/solution.py
@@ -48,7 +48,7 @@
     c_hbm, meas_hbm, rej_hbm, pair_hbm, fetch_hbm, g_hbm, m_hbm, v_hbm,
     go_ref, mo_ref, vo_ref, res_ref,
     c_ref, meas_ref, rej_ref, pair_ref, fetch_ref, g_ref, m_ref, v_ref, in_sem,
-    csend, crecv, pick, gsplit, grads, state_g, state_m, state_v,
+    csend, crecv, pick, gsplit, early, grads, state_g, state_m, state_v,
     gpiece, zg, zp, rsn, rsc, rsh, accp, rsp, tots, xs, xr, ressend, resrecv,
     c_ss, c_rs, a1_ss, a1_rs, a2_ss, a2_rs, r1_ss, r1_rs, rc_ss, rc_rs, rh_ss, rh_rs, r2_ss, r2_rs, x_ss, x_rs, o_ss, o_rs,
 ):
@@ -62,6 +62,12 @@
     def device(k, dz=0, dx=0):
         k = NS - 1 if k is None else k
         return (column_of[k] + plane_at[dz], (x + dx) & (NX - 1) if dx else x)
+
+    toward = jnp.where((z >= 1) & (z <= NZ // 2), 0, 1)
+
+    def device_along(k, direction, planes):
+        k = NS - 1 if k is None else k
+        return (column_of[k] + 2 * ((z + planes * (2 * direction - 1)) & (NZ - 1)), x)
 
     barrier = pltpu.get_barrier_semaphore()
     partners = [device(k, j) for j in CENTRES for k in range(NS) if j or k < NS - 1]
@@ -172,9 +178,9 @@
         for i, n in enumerate(STEPS):
             near_copy(0, 2, 2 + 2 * i, 0, n)
 
-    def gains_in(it):
-        waiter(zg.at[it, pl.ds(10, 6)], a2_ss.at[it], a2_rs.at[it, 1]).wait_recv()
-        waiter(zg.at[it, pl.ds(2, 5)], a2_ss.at[it], a2_rs.at[it, 0]).wait_recv()
+    def gains_in(it, part):
+        slots = pl.ds(10, 6) if part else pl.ds(2, 5)
+        waiter(zg.at[it, slots], a2_ss.at[it], a2_rs.at[it, part]).wait_recv()
 
     def gains_sent(it):
         waiter(zg.at[it, pl.ds(0, 4)], a1_ss.at[it], a1_rs.at[it, 0]).wait_send()
@@ -268,16 +274,24 @@
 
     for it in range(ITERS):
         last = it == ITERS - 1
-        gains_in(it)
-        for t in range(4):
+        def split(t):
             block = zg[it, 4 * t : 4 * t + 4].reshape(128, 128).T
             high = block.astype(BF16)
             gsplit[0:128, 128 * t : 128 * t + 128] = high
             gsplit[128:256, 128 * t : 128 * t + 128] = (block - high.astype(F32)).astype(BF16)
 
+        gains_in(it, 1)
+        split(2)
+        split(3)
+        for i in range(NS):
+            both = jnp.dot(gsplit[:, 256:512], pick[256:512, 256 * i : 256 * i + 256], preferred_element_type=F32)
+            early[i] = both[0:128] + both[128:256]
+        gains_in(it, 0)
+        split(0)
+        split(1)
         for i, source in enumerate(sources):
-            both = jnp.dot(gsplit[...], pick[:, 256 * i : 256 * i + 256], preferred_element_type=F32)
-            both = both[0:128] + both[128:256]
+            both = jnp.dot(gsplit[:, 0:256], pick[0:256, 256 * i : 256 * i + 256], preferred_element_type=F32)
+            both = both[0:128] + both[128:256] + early[i]
             ga, gb = both[0:64, 0:128], both[64:128, 0:128]
             gc, gd = both[0:64, 128:256], both[64:128, 128:256]
             cr, ci = crecv[source, 0:64, :], crecv[source, 64:128, :]
@@ -313,15 +327,17 @@
             zp[it, begin:end, :] = both[:, 0:128] + both[:, 128:256]
 
         station_sums(0, 32 * FIRST)
-        for i, n in enumerate(STEPS):
-            remote(zp.at[it, pl.ds(64 + 64 * i, 64)], rsn.at[it, i], r1_ss.at[it], r1_rs.at[it], device(None, -n)).start()
         for h in range(2):
             remote(
                 zp.at[it, pl.ds(32 * OPPOSITE + 16 * h, 16)], rsh.at[it, h], rh_ss.at[it], rh_rs.at[it], device(None, 4 * h - 2)
             ).start()
+        for i in (toward, 1 - toward):
+            rows = pl.ds(pl.multiple_of(64 + 64 * i, 32), 64)
+            remote(zp.at[it, rows], rsn.at[it, i], r1_ss.at[it], r1_rs.at[it], device_along(None, i, 1)).start()
         station_sums(32 * FIRST, ROWS)
-        for i, n in enumerate(STEPS):
-            remote(zp.at[it, pl.ds(320 + 96 * i, 96)], rsc.at[it, i], rc_ss.at[it], rc_rs.at[it], device(None, -n)).start()
+        for i in (toward, 1 - toward):
+            rows = pl.ds(pl.multiple_of(320 + 96 * i, 32), 96)
+            remote(zp.at[it, rows], rsc.at[it, i], rc_ss.at[it], rc_rs.at[it], device_along(None, i, 1)).start()
         if last:
             for k in range(NS - 1):
                 remote(ressend.at[mates[k]], resrecv.at[s], o_ss, o_rs, device(k)).start()
@@ -332,24 +348,35 @@
         near = waiter(rsn.at[it], r1_ss.at[it], r1_rs.at[it])
         half = waiter(rsh.at[it], rh_ss.at[it], rh_rs.at[it])
         own = waiter(rsc.at[it], rc_ss.at[it], rc_rs.at[it])
-        def far_out(j, acc):
+        def far_store(j, acc):
             for k in range(NS):
                 accp[it, j, k] = acc[4 * k : 4 * k + 4]
-            for k in [*range(NS - 1)] + ([None] if CENTRES[j] else []):
-                to = s if k is None else mates[k]
-                remote(
-                    accp.at[it, j, to], rsp.at[it, j, s], r2_ss.at[it], r2_rs.at[it, (0, 3, 1, 1, 2)[j]], device(k, CENTRES[j])
-                ).start()
+
+        def far_out(planes):
+            first = 0 if planes == 6 else 2
+            for side in (toward, 1 - toward):
+                j = first + side
+                for k in [*range(NS - 1), None]:
+                    to = s if k is None else mates[k]
+                    remote(
+                        accp.at[it, j, to], rsp.at[it, j, s], r2_ss.at[it], r2_rs.at[it, j], device_along(k, side, planes)
+                    ).start()
 
         near.wait_recv()
         half.wait_recv()
         acc = zp[it, 0:64, :] + rsn[it, 0] + rsn[it, 1]
-        far_out(0, jnp.concatenate([acc[0:16] + rsh[it, 0], acc[16:32]], axis=0))
-        far_out(1, jnp.concatenate([acc[32:48], acc[48:64] + rsh[it, 1]], axis=0))
+        far_store(0, jnp.concatenate([acc[0:16] + rsh[it, 0], acc[16:32]], axis=0))
+        far_store(1, jnp.concatenate([acc[32:48], acc[48:64] + rsh[it, 1]], axis=0))
+        far_out(6)
         own.wait_recv()
         acc = zp[it, 32 * FIRST : 32 * FIRST + 96, :] + rsc[it, 0] + rsc[it, 1]
         for j in (2, 3, 4):
-            far_out(j, acc[32 * j - 64 : 32 * j - 32])
+            far_store(j, acc[32 * j - 64 : 32 * j - 32])
+        far_out(3)
+        for k in range(NS - 1):
+            remote(
+                accp.at[it, NC - 1, mates[k]], rsp.at[it, NC - 1, s], r2_ss.at[it], r2_rs.at[it, NC - 1], device(k)
+            ).start()
         rsp[it, NC - 1, s] = accp[it, NC - 1, s]
         near.wait_send()
         half.wait_send()
@@ -361,12 +388,13 @@
             for k in range(NS):
                 for ri in range(2):
                     res_ref[ri, 2 * k : 2 * k + 2, :] = resrecv[k, 2 * ri : 2 * ri + 2, :]
-        waiter(rsp.at[it, NC - 1, pl.ds(0, NS - 1)], r2_ss.at[it], r2_rs.at[it, 2]).wait_recv()
-        waiter(rsp.at[it, pl.ds(2, 2)], r2_ss.at[it], r2_rs.at[it, 1]).wait_recv()
+        waiter(rsp.at[it, NC - 1, pl.ds(0, NS - 1)], r2_ss.at[it], r2_rs.at[it, NC - 1]).wait_recv()
+        for j in (2, 3):
+            waiter(rsp.at[it, j], r2_ss.at[it], r2_rs.at[it, j]).wait_recv()
         for k in range(NS):
             tots[4 * k : 4 * k + 4, :] = rsp[it, 4, k] + rsp[it, 2, k] + rsp[it, 3, k]
         for j in (0, 1):
-            waiter(rsp.at[it, j], r2_ss.at[it], r2_rs.at[it, j and 3]).wait_recv()
+            waiter(rsp.at[it, j], r2_ss.at[it], r2_rs.at[it, j]).wait_recv()
         for k in range(NS):
             tots[4 * k : 4 * k + 4, :] += rsp[it, 0, k] + rsp[it, 1, k]
 
@@ -374,9 +402,8 @@
         tally = STEP + it + 1
         new_m = BETA_ONE * state_m[...] + (1.0 - BETA_ONE) * smoothed
         new_v = BETA_TWO * state_v[...] + (1.0 - BETA_TWO) * smoothed * smoothed
-        first_hat = new_m / (1.0 - BETA_ONE**tally)
-        second_hat = new_v / (1.0 - BETA_TWO**tally)
-        new_g = state_g[...] - LEARN_RATE * first_hat / (jnp.sqrt(second_hat) + ADAM_EPSILON)
+        rate = LEARN_RATE / (1.0 - BETA_ONE**tally)
+        new_g = state_g[...] - rate * new_m / (jnp.sqrt(new_v * (1.0 / (1.0 - BETA_TWO**tally))) + ADAM_EPSILON)
         if last:
             from_pieces(new_g, go_ref)
             from_pieces(new_m, mo_ref)
@@ -427,6 +454,7 @@
             buf((NS, CROWS, NBL), F32),
             buf((ROWS, 2 * NBL * NS), BF16),
             buf((256, ROWS), BF16),
+            buf((NS, 128, 256), F32),
             buf((256, 2 * NBL * NS), BF16),
             buf((32, 128), F32),
             buf((32, 128), F32),
@@ -450,7 +478,7 @@
             sem((ITERS,)), sem((ITERS,)),
             sem((ITERS,)), sem((ITERS,)),
             sem((ITERS,)), sem((ITERS,)),
-            sem((ITERS,)), sem((ITERS, 4)),
+            sem((ITERS,)), sem((ITERS, NC)),
             sem((ITERS,)), sem((ITERS,)),
             sem, sem,
         ],

time: 75.4 us -> 74.4 us (0.987)
  Pallas kernels: 74.6 us -> 73.6 us
    pallas_call x1, Pallas kernels: 73.9 us -> 72.9 us  [on_device(): pl.pallas_call(kernel, out_shape=out, in_specs=[hbm] * 8, out_specs=[vmem...]
where the time goes in v4:
time: 74.4 us; the launch traced here: 74.2 us
  Pallas kernels  73.6 us (99%)
    pallas_call x1, Pallas kernels, on_device(): pl.pallas_call(kernel, out_shape=out, in_specs=[hbm] * 8, out_specs=[vmem...  72.9 us

profile of v4, /device:TPU:1, one launch (start us, length us, event | category | flops | bytes accessed | tf_op | source)
XLA Modules:
  0.0 74.2 jit_solution(12186434864269054902)
XLA Ops:
  0.6 72.9 %calibrate.1 = (f32[2,4,512]{2,1,0:T(4,128)S(1)}, f32[2,4,512]{2,1,0:T(4,128)S(1)}, f32[2,4,512]{2,1,0:T(4,128)S(1)}, f32[2,16,128]{2,1,0:T(8,128)S(1)}) custom-call(bf16[2,128,512]{2,1,0:T(8,128)(2,1)} %c_hbm.1, f32[2,16,128]{2,1,0:T(8,128)} %bitcast.6, s32[16,128]{1,0:T(8,128)} %bitcast.8, s32[2,128]{1,0:T(2,128)} %bitcast.9, s32[64,128]{1,0:T(8,128)} %bitcast.5, ...), custom_call_target="tpu_custom_call" | custom-call | flops 4000000000 | bytes 1048576 | tf_op jit(solution)/shard_map/calibrate/pallas_call | solution.py:445
  73.5 0.7 store.1

commit v5 on v4

--- a/solution.py
+++ b/solution.py
@@ -49,7 +49,7 @@
     go_ref, mo_ref, vo_ref, res_ref,
     c_ref, meas_ref, rej_ref, pair_ref, fetch_ref, g_ref, m_ref, v_ref, in_sem,
     csend, crecv, pick, gsplit, early, grads, state_g, state_m, state_v,
-    gpiece, zg, zp, rsn, rsc, rsh, accp, rsp, tots, xs, xr, ressend, resrecv,
+    gpiece, zg, zp, rsn, rsc, rsh, accp, rsp, xs, xr, ressend, resrecv,
     c_ss, c_rs, a1_ss, a1_rs, a2_ss, a2_rs, r1_ss, r1_rs, rc_ss, rc_rs, rh_ss, rh_rs, r2_ss, r2_rs, x_ss, x_rs, o_ss, o_rs,
 ):
     bl, x = lax.axis_index("bl"), lax.axis_index("ch")
@@ -109,8 +109,7 @@
 
     loads[0].wait()
     to_pieces(g_ref, state_g)
-    for k in range(NS):
-        gpiece[0, k] = state_g[4 * k : 4 * k + 4, :]
+    gpiece[0] = state_g[...]
 
     for load in loads[1:5]:
         load.wait()
@@ -145,16 +144,20 @@
 
     pl.semaphore_wait(barrier, len(partners))
 
+    def rows_of(device_in_plane):
+        return pl.ds(pl.multiple_of(4 * device_in_plane, 4), 4)
+
     def waiter(ref, send_sem, recv_sem):
         return remote(ref, ref, send_sem, recv_sem, device(0))
 
     def gains_out(it):
-        for j in range(NC):
-            for k in [*range(NS - 1)] + ([None] if CENTRES[j] else []):
+        for pair in ((0, 1), (2, 3), (4,)):
+            for k in [*range(NS - 1)] + ([None] if pair[0] < 4 else []):
                 to = s if k is None else mates[k]
-                remote(
-                    gpiece.at[it, to], zg.at[it, BACK[j], s], a1_ss.at[it], a1_rs.at[it, GROUP[j]], device(k, CENTRES[j])
-                ).start()
+                for j in pair:
+                    remote(
+                        gpiece.at[it, rows_of(to)], zg.at[it, BACK[j], rows_of(s)], a1_ss.at[it], a1_rs.at[it, GROUP[j]], device(k, CENTRES[j])
+                    ).start()
 
     def gains_on(it):
         def near_copy(src, width, dst, part, n):
@@ -162,8 +165,8 @@
                 zg.at[it, pl.ds(src, width)], zg.at[it, pl.ds(dst, width)], a2_ss.at[it], a2_rs.at[it, part], device(None, n)
             ).start()
 
-        zg[it, OWN, s] = gpiece[it, s]
-        waiter(zg.at[it, OWN, pl.ds(0, NS - 1)], a1_ss.at[it], a1_rs.at[it, 3]).wait_recv()
+        zg[it, OWN, rows_of(s), :] = gpiece[it, rows_of(s), :]
+        waiter(zg.at[it, OWN, pl.ds(0, 28)], a1_ss.at[it], a1_rs.at[it, 3]).wait_recv()
         for i, n in enumerate(STEPS):
             near_copy(OWN, 1, 12 + 3 * i, 1, n)
         waiter(zg.at[it, pl.ds(7, 2)], a1_ss.at[it], a1_rs.at[it, 2]).wait_recv()
@@ -171,7 +174,7 @@
             near_copy(7, 2, 10 + 3 * i, 1, n)
         for h in range(2):
             waiter(zg.at[it, h], a1_ss.at[it], a1_rs.at[it, h]).wait_recv()
-            half = pl.ds(4 * h, 4)
+            half = pl.ds(16 * h, 16)
             remote(
                 zg.at[it, h, half], zg.at[it, OPPOSITE, half], a2_ss.at[it], a2_rs.at[it, 0], device(None, 2 - 4 * h)
             ).start()
@@ -184,7 +187,7 @@
 
     def gains_sent(it):
         waiter(zg.at[it, pl.ds(0, 4)], a1_ss.at[it], a1_rs.at[it, 0]).wait_send()
-        waiter(zg.at[it, OWN, pl.ds(0, NS - 1)], a1_ss.at[it], a1_rs.at[it, 0]).wait_send()
+        waiter(zg.at[it, OWN, pl.ds(0, 28)], a1_ss.at[it], a1_rs.at[it, 0]).wait_send()
         waiter(zg.at[it, pl.ds(0, 11)], a2_ss.at[it], a2_rs.at[it, 0]).wait_send()
 
     gains_out(0)
@@ -242,8 +245,7 @@
     def swap(value):
         return jnp.where((lax.broadcasted_iota(I32, value.shape, 1) & 32) != 0, pltpu.roll(value, 32, 1), pltpu.roll(value, 96, 1))
 
-    def smooth(it):
-        total = tots[...]
+    def smooth(it, total):
         swapped = swap(total)
         edge = total * edge_same + swapped * edge_other
         edge = (edge[0:8] + edge[8:16]) + (edge[16:24] + edge[24:32])
@@ -349,8 +351,7 @@
         half = waiter(rsh.at[it], rh_ss.at[it], rh_rs.at[it])
         own = waiter(rsc.at[it], rc_ss.at[it], rc_rs.at[it])
         def far_store(j, acc):
-            for k in range(NS):
-                accp[it, j, k] = acc[4 * k : 4 * k + 4]
+            accp[it, j] = acc
 
         def far_out(planes):
             first = 0 if planes == 6 else 2
@@ -359,7 +360,7 @@
                 for k in [*range(NS - 1), None]:
                     to = s if k is None else mates[k]
                     remote(
-                        accp.at[it, j, to], rsp.at[it, j, s], r2_ss.at[it], r2_rs.at[it, j], device_along(k, side, planes)
+                        accp.at[it, j, rows_of(to)], rsp.at[it, j, rows_of(s)], r2_ss.at[it], r2_rs.at[it, j], device_along(k, side, planes)
                     ).start()
 
         near.wait_recv()
@@ -375,9 +376,9 @@
         far_out(3)
         for k in range(NS - 1):
             remote(
-                accp.at[it, NC - 1, mates[k]], rsp.at[it, NC - 1, s], r2_ss.at[it], r2_rs.at[it, NC - 1], device(k)
+                accp.at[it, NC - 1, rows_of(mates[k])], rsp.at[it, NC - 1, rows_of(s)], r2_ss.at[it], r2_rs.at[it, NC - 1], device(k)
             ).start()
-        rsp[it, NC - 1, s] = accp[it, NC - 1, s]
+        rsp[it, NC - 1, rows_of(s), :] = accp[it, NC - 1, rows_of(s), :]
         near.wait_send()
         half.wait_send()
         own.wait_send()
@@ -388,17 +389,14 @@
             for k in range(NS):
                 for ri in range(2):
                     res_ref[ri, 2 * k : 2 * k + 2, :] = resrecv[k, 2 * ri : 2 * ri + 2, :]
-        waiter(rsp.at[it, NC - 1, pl.ds(0, NS - 1)], r2_ss.at[it], r2_rs.at[it, NC - 1]).wait_recv()
+        waiter(rsp.at[it, NC - 1, pl.ds(0, 28)], r2_ss.at[it], r2_rs.at[it, NC - 1]).wait_recv()
         for j in (2, 3):
             waiter(rsp.at[it, j], r2_ss.at[it], r2_rs.at[it, j]).wait_recv()
-        for k in range(NS):
-            tots[4 * k : 4 * k + 4, :] = rsp[it, 4, k] + rsp[it, 2, k] + rsp[it, 3, k]
+        total = rsp[it, 4] + rsp[it, 2] + rsp[it, 3]
         for j in (0, 1):
             waiter(rsp.at[it, j], r2_ss.at[it], r2_rs.at[it, j]).wait_recv()
-        for k in range(NS):
-            tots[4 * k : 4 * k + 4, :] += rsp[it, 0, k] + rsp[it, 1, k]
-
-        smoothed = smooth(it)
+        total = total + rsp[it, 0] + rsp[it, 1]
+        smoothed = smooth(it, total)
         tally = STEP + it + 1
         new_m = BETA_ONE * state_m[...] + (1.0 - BETA_ONE) * smoothed
         new_v = BETA_TWO * state_v[...] + (1.0 - BETA_TWO) * smoothed * smoothed
@@ -409,14 +407,13 @@
             from_pieces(new_m, mo_ref)
             from_pieces(new_v, vo_ref)
         else:
-            for k in range(NS):
-                gpiece[it + 1, k] = new_g[4 * k : 4 * k + 4]
+            gpiece[it + 1] = new_g
             gains_out(it + 1)
             state_g[...] = new_g
             state_m[...] = new_m
             state_v[...] = new_v
         waiter(rsp.at[it, pl.ds(0, NC - 1)], r2_ss.at[it], r2_rs.at[it, 0]).wait_send()
-        waiter(rsp.at[it, NC - 1, pl.ds(0, NS - 1)], r2_ss.at[it], r2_rs.at[it, 2]).wait_send()
+        waiter(rsp.at[it, NC - 1, pl.ds(0, 28)], r2_ss.at[it], r2_rs.at[it, 2]).wait_send()
         waiter(xr.at[it], x_ss.at[it], x_rs.at[it]).wait_send()
         if not last:
             gains_on(it + 1)
@@ -459,15 +456,14 @@
             buf((32, 128), F32),
             buf((32, 128), F32),
             buf((32, 128), F32),
-            buf((ITERS, NS, 4, 128), F32),
-            buf((ITERS, NZ, NS, 4, 128), F32),
+            buf((ITERS, 32, 128), F32),
+            buf((ITERS, NZ, 32, 128), F32),
             buf((ITERS, ROWS, 128), F32),
             buf((ITERS, 2, 64, 128), F32),
             buf((ITERS, 2, 96, 128), F32),
             buf((ITERS, 2, 16, 128), F32),
-            buf((ITERS, NC, NS, 4, 128), F32),
-            buf((ITERS, NC, NS, 4, 128), F32),
-            buf((32, 128), F32),
+            buf((ITERS, NC, 32, 128), F32),
+            buf((ITERS, NC, 32, 128), F32),
             buf((ITERS, 4, 128), F32),
             buf((ITERS, 3, 4, 128), F32),
             buf((NS, 4, 128), F32),

time: 74.4 us -> 74.3 us (level)
  no operation moved by 1% of the time
where the time goes in v5:
time: 74.3 us; the launch traced here: 74.1 us
  Pallas kernels  73.5 us (99%)
    pallas_call x1, Pallas kernels, on_device(): pl.pallas_call(kernel, out_shape=out, in_specs=[hbm] * 8, out_specs=[vmem...  72.8 us

profile of v5, /device:TPU:1, one launch (start us, length us, event | category | flops | bytes accessed | tf_op | source)
XLA Modules:
  0.0 74.1 jit_solution(10313513811187520523)
XLA Ops:
  0.6 72.8 %calibrate.1 = (f32[2,4,512]{2,1,0:T(4,128)S(1)}, f32[2,4,512]{2,1,0:T(4,128)S(1)}, f32[2,4,512]{2,1,0:T(4,128)S(1)}, f32[2,16,128]{2,1,0:T(8,128)S(1)}) custom-call(bf16[2,128,512]{2,1,0:T(8,128)(2,1)} %c_hbm.1, f32[2,16,128]{2,1,0:T(8,128)} %bitcast.6, s32[16,128]{1,0:T(8,128)} %bitcast.8, s32[2,128]{1,0:T(2,128)} %bitcast.9, s32[64,128]{1,0:T(8,128)} %bitcast.5, ...), custom_call_target="tpu_custom_call" | custom-call | flops 4000000000 | bytes 1048576 | tf_op jit(solution)/shard_map/calibrate/pallas_call | solution.py:442
  73.5 0.7 store.1
